TPU v7x, 256 devices: a whole 4x4x8 slice. The times are simulated.
256 devices in a mesh: outer: 8 (over z), inner: 32 (over x, y, core).
Axes of the slice: x: 4, y: 4, z: 8, core: 2. Of those that a mesh axis runs over, the one named last changes fastest.
Arguments:
- b_leaf: float32 [65536, 64], P(('outer', 'inner')), may hold values from -6 to 6
- b_sep: float32 [2048, 64], P(('outer', 'inner')), may hold values from -6 to 6
- b_root: float32 [2048, 64], P(('outer', 'inner')), may hold values from -6 to 6
- leaf_linv: float32 [65536, 256], P(('outer', 'inner')), as said below
- leaf_uinv: float32 [65536, 256], P(('outer', 'inner')), as said below
- leaf_lower: float32 [65536, 256], P(('outer', 'inner')), as said below
- leaf_upper: float32 [65536, 256], P(('outer', 'inner')), as said below
- sep_rows: int32 [256, 256], P(('outer', 'inner')), may hold values from 0 to 255, as said below
- sep_linv: float32 [2048, 256], P(('outer', 'inner')), as said below
- sep_uinv: float32 [2048, 256], P(('outer', 'inner')), as said below
- sep_lower: float32 [2048, 2048], P(None, ('outer', 'inner')), as said below
- sep_upper: float32 [2048, 2048], P(('outer', 'inner')), as said below
- root_linv: float32 [2048, 2048], P(('outer', 'inner')), as said below
- root_uinv: float32 [2048, 2048], P(('outer', 'inner')), as said below
- basis_leaf: float32 [65536, 512], P(('outer', 'inner')), as said below
- basis_sep: float32 [2048, 512], P(('outer', 'inner')), as said below
- basis_root: float32 [2048, 512], P(('outer', 'inner')), as said below
- g_blocks: float32 [262144, 128], P(('outer', 'inner')), may hold values from -0.25 to 0.25
- c_blocks: float32 [262144, 128], P(('outer', 'inner')), may hold values from -0.25 to 0.25
- block_cols: int32 [512, 4], P(('outer', 'inner')), may hold values from 0 to 1
Outputs:
- v_leaf: float32 [65536, 64], P(('outer', 'inner'))
- v_sep: float32 [2048, 64], P(('outer', 'inner'))
- v_root: float32 [2048, 64], P(('outer', 'inner'))
- coefficients: float32 [512, 64], replicated
- reduced_g: float32 [64, 64], replicated
- reduced_c: float32 [64, 64], replicated
Inputs may be any that keep to these rules, and one draw needn't show every extreme that they name: `sep_rows`: each row holds 256 distinct numbers; every row names 0 and 255. `leaf_linv`: lower triangular in each diagonal block of the stack, nonzero diagonal. `leaf_uinv`: upper triangular in each diagonal block of the stack, nonzero diagonal. `sep_linv`: lower triangular in each block of 256 rows, nonzero diagonal. `sep_uinv`: upper triangular in each block of 256 rows, nonzero diagonal. `root_linv`: lower triangular, nonzero diagonal. `root_uinv`: upper triangular, nonzero diagonal. `leaf_lower`: entries of order one over the square root of 256. `leaf_upper`: entries of order one over the square root of 256. `sep_lower`: entries of order one over the square root of the number of its columns. `sep_upper`: entries of order one over the square root of 2048. basis_leaf, basis_sep and basis_root stacked by rows form Q with Q^T Q = 69632 I up to float32 rounding. `basis_sep`: part of the stacked Q described with basis_leaf. `basis_root`: part of the stacked Q described with basis_leaf.
All inputs are finite; a program needn't handle non-finite values.
Results may differ from a plain program's by a relative error of at most 0.0003.
Values sent between devices are 32-bit elements; how exact they have to be, the bound alone decides.
A program may use at most 64 MiB of HBM per device.

v0:
```python
import jax
import jax.numpy as jnp
from jax import lax
from jax.sharding import PartitionSpec as P


def matmul_exact(left, right):
    return jnp.dot(left, right, precision=lax.Precision.HIGHEST, preferred_element_type=jnp.float32)


def contract_rows(left, right):
    return lax.dot_general(
        left,
        right,
        (((0,), (0,)), ((), ())),
        precision=lax.Precision.HIGHEST,
        preferred_element_type=jnp.float32,
    )


def shards(
    b_leaf,
    b_sep,
    b_root,
    leaf_linv,
    leaf_uinv,
    leaf_lower,
    leaf_upper,
    sep_rows,
    sep_linv,
    sep_uinv,
    sep_lower,
    sep_upper,
    root_linv,
    root_uinv,
    basis_leaf,
    basis_sep,
    basis_root,
    g_blocks,
    c_blocks,
    block_cols,
):
    ports = b_leaf.shape[1]
    sep_local = b_sep.shape[0]
    root_local = b_root.shape[0]
    sep_width = sep_linv.shape[1]
    selector = (sep_rows[0][:, None] == jnp.arange(sep_width, dtype=jnp.int32)[None, :]).astype(
        jnp.float32
    )
    y_leaf = matmul_exact(leaf_linv, b_leaf)
    contrib = matmul_exact(leaf_lower, y_leaf)
    t_sep = lax.psum_scatter(
        contract_rows(selector, contrib), "inner", scatter_dimension=0, tiled=True
    )
    sep_whole = lax.all_gather(b_sep - t_sep, "inner", axis=0, tiled=True)
    y_sep = matmul_exact(sep_linv, sep_whole)
    t_root = lax.psum_scatter(
        matmul_exact(sep_lower, y_sep), ("outer", "inner"), scatter_dimension=0, tiled=True
    )
    root_rhs = lax.all_gather(b_root - t_root, ("outer", "inner"), axis=0, tiled=True)
    y_root = matmul_exact(root_linv, root_rhs)
    y_root_all = lax.all_gather(y_root, ("outer", "inner"), axis=0, tiled=True)
    x_root = matmul_exact(root_uinv, y_root_all)
    x_root_all = lax.all_gather(x_root, ("outer", "inner"), axis=0, tiled=True)
    z_sep = y_sep - matmul_exact(sep_upper, x_root_all)
    z_sep_all = lax.all_gather(z_sep, "inner", axis=0, tiled=True)
    x_sep = matmul_exact(sep_uinv, z_sep_all)
    x_sep_all = lax.all_gather(x_sep, "inner", axis=0, tiled=True)
    coupled = matmul_exact(selector, x_sep_all)
    x_leaf = matmul_exact(leaf_uinv, y_leaf - matmul_exact(leaf_upper, coupled))
    node_count = float(
        lax.axis_size("outer") * lax.axis_size("inner") * (b_leaf.shape[0] + sep_local + root_local)
    )
    pieces_x = (x_leaf, x_sep, x_root)
    pieces_q = (basis_leaf, basis_sep, basis_root)
    projected = (
        contract_rows(basis_leaf, x_leaf)
        + contract_rows(basis_sep, x_sep)
        + contract_rows(basis_root, x_root)
    )
    coefficients = lax.psum(projected, ("outer", "inner")) / node_count
    cleaned = [
        values - matmul_exact(basis, coefficients) for basis, values in zip(pieces_q, pieces_x)
    ]
    local_gram = (
        contract_rows(cleaned[0], cleaned[0])
        + contract_rows(cleaned[1], cleaned[1])
        + contract_rows(cleaned[2], cleaned[2])
    )
    gram_matrix = lax.psum(local_gram, ("outer", "inner")) / node_count
    chol_lower = jnp.linalg.cholesky(gram_matrix)
    inverse_lower = lax.linalg.triangular_solve(
        chol_lower, jnp.eye(ports, dtype=jnp.float32), left_side=True, lower=True
    )
    v_leaf = matmul_exact(cleaned[0], inverse_lower.T)
    v_sep = matmul_exact(cleaned[1], inverse_lower.T)
    v_root = matmul_exact(cleaned[2], inverse_lower.T)
    block_rows = block_cols.shape[0]
    stored = block_cols.shape[1]
    block_size = g_blocks.shape[1]
    blocked = v_leaf.reshape(block_rows, block_size, ports)
    picked = blocked[block_cols]
    g_tiles = g_blocks.reshape(block_rows, stored, block_size, block_size)
    c_tiles = c_blocks.reshape(block_rows, stored, block_size, block_size)
    g_image = jnp.einsum("rwij,rwjp->rip", g_tiles, picked, precision=lax.Precision.HIGHEST)
    c_image = jnp.einsum("rwij,rwjp->rip", c_tiles, picked, precision=lax.Precision.HIGHEST)
    g_local = jnp.einsum("rip,riq->pq", blocked, g_image, precision=lax.Precision.HIGHEST)
    c_local = jnp.einsum("rip,riq->pq", blocked, c_image, precision=lax.Precision.HIGHEST)
    g_summed, c_summed = lax.psum((g_local, c_local), ("outer", "inner"))
    return (v_leaf, v_sep, v_root, coefficients, g_summed / node_count, c_summed / node_count)


def solution(mesh):
    return jax.shard_map(
        shards,
        mesh=mesh,
        in_specs=(
            P(("outer", "inner"), None),
            P(("outer", "inner"), None),
            P(("outer", "inner"), None),
            P(("outer", "inner"), None),
            P(("outer", "inner"), None),
            P(("outer", "inner"), None),
            P(("outer", "inner"), None),
            P(("outer", "inner"), None),
            P(("outer", "inner"), None),
            P(("outer", "inner"), None),
            P(None, ("outer", "inner")),
            P(("outer", "inner"), None),
            P(("outer", "inner"), None),
            P(("outer", "inner"), None),
            P(("outer", "inner"), None),
            P(("outer", "inner"), None),
            P(("outer", "inner"), None),
            P(("outer", "inner"), None),
            P(("outer", "inner"), None),
            P(("outer", "inner"), None),
        ),
        out_specs=(
            P(("outer", "inner"), None),
            P(("outer", "inner"), None),
            P(("outer", "inner"), None),
            P(),
            P(),
            P(),
        ),
        check_vma=False,
    )
```

profile of v0, /device:TPU:1, one launch (start us, length us, event | category | flops | bytes accessed | tf_op | source)
XLA Modules:
  0.0 1057.3 jit_solution(8577901284034292284)
XLA Ops:
  7.2 1.4 fusion.16
  9.7 1.0 fusion.8
  12.7 112.8 %all-reduce.9.cloned.1.call-done = f32[256,64]{1,0:T(8,128)} async-done(((f32[256,64]{1,0:T(8,128)}), f32[256,64]{1,0:T(8,128)}) %all-reduce.9.cloned.1.call-update) | async-done | bytes 65552
  125.5 0.7 dynamic-slice_subtract_fusion.1
  126.2 25.7 %all_gather.18 = f32[256,64]{1,0:T(8,128)S(1)} all-gather(f32[8,64]{1,0:T(8,128)S(1)} %dynamic-slice_subtract_fusion.1), channel_id=1, replica_groups=mesh['outer'=8,'inner'=32] {'inner'}, dimensions={0}, use_global_device_ids=true | all-gather | bytes 67584 | tf_op jit(solution)/shard_map/all_gather | solution.py:55
  153.3 1.3 copy.47
  155.4 251.8 %all-reduce.11.cloned.1.call-done = f32[2048,64]{1,0:T(8,128)} async-done(((f32[2048,64]{1,0:T(8,128)}), f32[2048,64]{1,0:T(8,128)}) %all-reduce.11.cloned.1.call-update) | async-done | bytes 524304
  407.2 0.7 dynamic-slice_subtract_fusion
  407.9 63.2 %all_gather.19 = f32[2048,64]{1,0:T(8,128)S(1)} all-gather(f32[8,64]{1,0:T(8,128)S(1)} %dynamic-slice_subtract_fusion), channel_id=1, replica_groups=mesh['outer'=8,'inner'=32] {'outer','inner'}, dimensions={0}, use_global_device_ids=true | all-gather | bytes 526336 | tf_op jit(solution)/shard_map/all_gather | solution.py:60
  471.7 60.2 %all_gather.20 = f32[2048,64]{1,0:T(8,128)S(1)} all-gather(f32[8,64]{1,0:T(8,128)S(1)} %convolution_bitcast_fusion.8), channel_id=1, replica_groups=mesh['outer'=8,'inner'=32] {'outer','inner'}, dimensions={0}, use_global_device_ids=true | all-gather | bytes 526336 | tf_op jit(solution)/shard_map/all_gather | solution.py:62
  532.6 60.4 %all_gather.21 = f32[2048,64]{1,0:T(8,128)S(1)} all-gather(f32[8,64]{1,0:T(8,128)S(1)} %bitcast.121), channel_id=1, replica_groups=mesh['outer'=8,'inner'=32] {'outer','inner'}, dimensions={0}, use_global_device_ids=true | all-gather | bytes 526336 | tf_op jit(solution)/shard_map/all_gather | solution.py:64
  593.7 23.3 %all_gather.22 = f32[256,64]{1,0:T(8,128)S(1)} all-gather(f32[8,64]{1,0:T(8,128)S(1)} %fusion.5), channel_id=1, replica_groups=mesh['outer'=8,'inner'=32] {'inner'}, dimensions={0}, use_global_device_ids=true | all-gather | bytes 67584 | tf_op jit(solution)/shard_map/all_gather | solution.py:66
  617.2 23.0 %all_gather.23 = f32[256,64]{1,0:T(8,128)S(1)} all-gather(f32[8,64]{1,0:T(8,128)S(1)} %bitcast.122), channel_id=1, replica_groups=mesh['outer'=8,'inner'=32] {'inner'}, dimensions={0}, use_global_device_ids=true | all-gather | bytes 67584 | tf_op jit(solution)/shard_map/all_gather | solution.py:68
  642.0 1.1 fusion.1
  643.1 237.7 %all-reduce.7.cloned.1.call-done = f32[512,64]{0,1:T(8,128)} async-done(((f32[512,64]{0,1:T(8,128)}), f32[512,64]{0,1:T(8,128)}) %all-reduce.7.cloned.1.call-update) | async-done | bytes 131088 | tf_op jit(solution)/shard_map/psum | solution.py:81
  880.8 0.9 broadcast_multiply_fusion
  883.5 76.0 %psum.29 = f32[64,64]{0,1:T(8,128)S(1)} all-reduce(f32[64,64]{0,1:T(8,128)S(1)} %convolution_add_fusion.1), channel_id=1, replica_groups=mesh['outer'=8,'inner'=32] {'outer','inner'}, use_global_device_ids=true, to_apply=%region_3.0 | all-reduce | flops 4096 | bytes 32768 | tf_op jit(solution)/shard_map/psum | solution.py:90
  959.7 5.8 cholesky.17
  966.9 4.9 custom-call.6
  972.2 0.8 fusion.27
  973.0 0.8 fusion.26
  976.2 73.1 %all-reduce.2 = (f32[64,64]{0,1:T(8,128)S(1)}, f32[64,64]{0,1:T(8,128)S(1)}) all-reduce(f32[64,64]{0,1:T(8,128)S(1)} %convolution_bitcast_fusion.5, f32[64,64]{0,1:T(8,128)S(1)} %convolution_bitcast_fusion.4), channel_id=1, replica_groups=mesh['outer'=8,'inner'=32] {'outer','inner'}, use_global_device_ids=true, to_apply=%region_6.7 | all-reduce | flops 8192 | bytes 65536 | tf_op jit(solution)/shard_map/psum | solution.py:109
  1049.4 0.7 copy.57
  1050.1 0.7 copy.58
  (85 shorter events, 14.6 us)
Async XLA Ops:
  7.2 967.2 %copy-start = (f32[1024,128]{1,0:T(8,128)S(1)}, f32[1024,128]{1,0:T(8,128)}, u32[]{:S(2)}) copy-start(f32[1024,128]{1,0:T(8,128)} %param.38) | copy-start | bytes 1572868
  7.2 1.5 copy-start.6
  7.2 118.3 %all-reduce.9.cloned.1.call-start = ((), (), s32[]{:S(2)}) async-start(), calls=%async_computation.1 | async-start | bytes 262144
  9.0 0.7 copy-start.16
  10.8 396.5 %all-reduce.11.cloned.1.call-start = ((), (), s32[]{:S(2)}) async-start(), calls=%async_computation.2 | async-start | bytes 2097152
  10.8 0.7 copy-start.20
  11.5 114.0 %copy-start.17 = (f32[8,64]{1,0:T(8,128)S(1)}, f32[8,64]{1,0:T(8,128)}, u32[]{:S(2)}) copy-start(f32[8,64]{1,0:T(8,128)} %param.21) | copy-start | bytes 6148
  126.2 25.7 %copy-start.14 = (f32[8,256]{1,0:T(8,128)S(1)}, f32[8,256]{1,0:T(8,128)}, u32[]{:S(2)}) copy-start(f32[8,256]{1,0:T(8,128)} %param.28) | copy-start | bytes 24580
  151.8 0.8 copy-start.8
  154.7 0.7 copy-start.19
  154.7 252.5 %copy-start.18 = (f32[8,64]{1,0:T(8,128)S(1)}, f32[8,64]{1,0:T(8,128)}, u32[]{:S(2)}) copy-start(f32[8,64]{1,0:T(8,128)} %param.22) | copy-start | bytes 6148
  154.7 726.1 %all-reduce.7.cloned.1.call-start = ((), (), s32[]{:S(2)}) async-start(), calls=%async_computation | async-start | bytes 262144 | tf_op jit(solution)/shard_map/psum | solution.py:81
  407.9 63.2 %copy-start.9 = (f32[8,2048]{1,0:T(8,128)S(1)}, f32[8,2048]{1,0:T(8,128)}, u32[]{:S(2)}) copy-start(f32[8,2048]{1,0:T(8,128)} %param.32) | copy-start | bytes 196612
  471.7 60.2 %copy-start.10 = (f32[8,2048]{1,0:T(8,128)S(1)}, f32[8,2048]{1,0:T(8,128)}, u32[]{:S(2)}) copy-start(f32[8,2048]{1,0:T(8,128)} %param.33) | copy-start | bytes 196612
  532.6 60.4 %copy-start.11 = (f32[8,2048]{1,0:T(8,128)S(1)}, f32[8,2048]{1,0:T(8,128)}, u32[]{:S(2)}) copy-start(f32[8,2048]{1,0:T(8,128)} %param.31) | copy-start | bytes 196612
  593.7 23.3 %copy-start.15 = (f32[8,256]{1,0:T(8,128)S(1)}, f32[8,256]{1,0:T(8,128)}, u32[]{:S(2)}) copy-start(f32[8,256]{1,0:T(8,128)} %param.29) | copy-start | bytes 24580
  617.2 23.4 %copy-start.12 = (f32[8,512]{1,0:T(8,128)S(1)}, f32[8,512]{1,0:T(8,128)}, u32[]{:S(2)}) copy-start(f32[8,512]{1,0:T(8,128)} %param.35) | copy-start | bytes 49156
  640.2 0.7 copy-start.13
  640.2 1.0 copy-start.5
  640.6 1.1 copy-start.7
  640.9 1.1 copy-start.1
  881.8 0.8 copy-start.2
  972.2 3.8 copy-start.3
  974.3 1.0 copy-start.4
Sparse Core Ops, SparseCore 0:
  11.8 113.6 all-reduce.8
  154.8 252.3 all-reduce.10
  643.3 237.5 all-reduce.6
where the time goes:
time: 1060 us
  waiting for transfers between devices  602 us (57%)
  blocking collectives  405 us (38%)
  between operations  14.7 us (1%)
  other arithmetic  14.4 us (1%)
  matrix products  14 us (1%)
    unnamed x5, waiting for transfers between devices  365 us
    psum x1, waiting for transfers between devices, shards(): coefficients = lax.psum(projected, ('outer', 'inner')) / node_count  238 us
    psum x1, blocking collectives, shards(): gram_matrix = lax.psum(local_gram, ('outer', 'inner')) / node_count  76 us
    psum x1, blocking collectives, shards(): g_summed, c_summed = lax.psum((g_local, c_local), ('outer', 'inner'))  73.1 us
    all_gather x1, blocking collectives, shards(): lax.all_gather(b_root - t_root, ('outer', 'inner'), axis=0, tiled=True)  63.2 us
    all_gather x1, blocking collectives, shards(): x_root_all = lax.all_gather(x_root, ('outer', 'inner'), axis=0, tiled=True)  60.4 us
    all_gather x1, blocking collectives, shards(): y_root_all = lax.all_gather(y_root, ('outer', 'inner'), axis=0, tiled=True)  60.2 us
    all_gather x1, blocking collectives, shards(): sep_whole = lax.all_gather(b_sep - t_sep, 'inner', axis=0, tiled=True)  25.7 us
  transfers between devices with their start and end apart: 3, of which 3 were waited for; matrix products, arithmetic and copies ran while one was open for 0% of the time, Pallas kernels for 0%

commit v1 on v0

v1 whole, which is shorter than its diff:
```python
import functools

import jax
import jax.numpy as jnp
from jax import lax
from jax.experimental import pallas as pl
from jax.experimental.pallas import tpu as pltpu
from jax.sharding import PartitionSpec as P

MESH = pl.DeviceIdType.MESH
F32 = jnp.float32
NN = ((1,), (0,))
NT = ((1,), (1,))
TN = ((0,), (0,))
PIECES_P = 32
PIECES_K = 16


def mul(left, right, dims=NN):
    return lax.dot_general(
        left, right, (dims, ((), ())), precision=lax.Precision.HIGHEST, preferred_element_type=F32
    )


def wide(block):
    return jnp.concatenate([block, jnp.zeros_like(block)], axis=1)


def folded(block):
    half = block.shape[0] // 2
    return jnp.concatenate([block[:half], block[half:]], axis=1)


def unfolded_product(left, both):
    half = left.shape[1] // 2
    upper = mul(left[:, :half], both)
    lower = mul(left[:, half:], both)
    return upper[:, :64] + lower[:, 64:]


def inverse_factor(gram):
    row_ids = lax.broadcasted_iota(jnp.int32, (64, 64), 0)
    col_ids = lax.broadcasted_iota(jnp.int32, (64, 64), 1)
    start = jnp.concatenate([gram, (row_ids == col_ids).astype(F32)], axis=1)
    groups = tuple(start[8 * a : 8 * a + 8] for a in range(8))
    sub = lax.broadcasted_iota(jnp.int32, (8, 128), 0)

    def panel(p, groups):
        groups = list(groups)
        scale = jnp.zeros((8, 128), F32)
        for k in range(8):
            row = groups[0][k : k + 1, :]
            pivot = row[:, k : k + 1]
            scaled = row / pivot
            for a in range(8):
                factor = groups[a][:, k : k + 1]
                if a == 0:
                    factor = jnp.where(sub > k, jnp.broadcast_to(factor, (8, 128)), 0.0)
                else:
                    live = jnp.where(a + p < 8, 1.0, 0.0).astype(F32)
                    factor = jnp.broadcast_to(factor, (8, 128)) * live
                groups[a] = groups[a] - factor * scaled
            scale = jnp.where(sub == k, jnp.broadcast_to(lax.rsqrt(pivot), (8, 128)), scale)
        groups[0] = groups[0] * scale
        turned = [pltpu.roll(x, 120, 1) for x in groups]
        return tuple(turned[1:] + turned[:1])

    groups = lax.fori_loop(0, 8, panel, groups)
    return jnp.concatenate(groups, axis=0)[:, :64]


def by_owner(columns, n_outer, n_inner, out_ref):
    if n_inner * 8 != 256:
        moved = columns.reshape(8, n_outer, n_inner, 8).transpose(2, 0, 1, 3).reshape(n_inner, 8, n_outer * 8)
        out_ref[...] = jnp.concatenate(
            [moved, jnp.zeros((n_inner, 8, 128 - n_outer * 8), F32)], axis=2
        )
        return
    lane_group = lax.broadcasted_iota(jnp.int32, (8, 128), 1) // 8
    for m in range(2):
        shifted = []
        for o in range(n_outer):
            at = o * 256 + m * 128
            piece = columns[:, at : at + 128]
            shifted.append(pltpu.roll(piece, o * 8, 1) if o else piece)
        for ii in range(16):
            total = shifted[0]
            for o in range(1, n_outer):
                total = jnp.where(lane_group == (ii + o) % 16, shifted[o], total)
            out_ref[16 * m + ii] = pltpu.roll(total, 128 - ii * 8, 1) if ii else total


def kernel(
    n_outer,
    n_inner,
    b_t,
    b_sep,
    b_root,
    leaf_linv,
    leaf_uinv,
    leaf_lower,
    leaf_upper,
    sep_rows,
    sep_linv,
    sep_uinv,
    sep_lower_t,
    sep_upper,
    root_linv,
    root_uinv,
    basis_leaf,
    basis_sep,
    basis_root,
    g_blocks,
    c_blocks,
    block_cols,
    v_leaf_t,
    v_sep,
    v_root,
    coef_t,
    red_g,
    red_c,
    a_src,
    a_rcv,
    b_buf,
    sl_buf,
    su_buf,
    sp_src,
    sp_buf,
    l_buf,
    u_buf,
    rz_buf,
    d_buf,
    e_buf,
    f_buf,
    z_buf,
    p_src,
    p_rcv,
    pz_buf,
    pc_buf,
    k_src,
    k_rcv,
    kz_buf,
    kc_buf,
    q_all,
    hg,
    hc,
    send,
    recv,
):
    g = lax.axis_index("outer")
    i = lax.axis_index("inner")
    rb = n_outer * 8
    n_own = kc_buf.shape[0]
    stride = n_inner // n_own
    nodes = float(n_outer * n_inner * (basis_leaf.shape[0] + 16))
    A, B, SL, SU, SP, L, U, RZ, D, E_, F_, Z, PR, PZ, PC, KR, KZ, KC = range(18)

    def to_plane(phase, src, dst):
        def one(k, carry):
            peer = lax.rem(i + k, n_inner)
            pltpu.make_async_remote_copy(
                src_ref=src(peer, k),
                dst_ref=dst(peer, k),
                send_sem=send.at[phase],
                recv_sem=recv.at[phase],
                device_id=(g, peer),
                device_id_type=MESH,
            ).start()
            return carry

        lax.fori_loop(1, n_inner, one, 0)

    def to_column(phase, src, dst):
        def one(k, carry):
            peer = lax.rem(g + k, n_outer)
            pltpu.make_async_remote_copy(
                src_ref=src,
                dst_ref=dst,
                send_sem=send.at[phase],
                recv_sem=recv.at[phase],
                device_id=(peer, i),
                device_id_type=MESH,
            ).start()
            return carry

        lax.fori_loop(1, n_outer, one, 0)

    def arrived(phase, like):
        pltpu.make_async_copy(like, like, recv.at[phase]).wait()

    def sent(phase, like):
        pltpu.make_async_copy(like, like, send.at[phase]).wait()

    others = pl.ds(0, n_inner - 1)
    others_z = pl.ds(0, n_outer - 1)

    barrier = pltpu.get_barrier_semaphore()

    def greet_plane(k, carry):
        pl.semaphore_signal(
            barrier, inc=1, device_id=(g, lax.rem(i + k, n_inner)), device_id_type=MESH
        )
        return carry

    def greet_column(k, carry):
        pl.semaphore_signal(
            barrier, inc=1, device_id=(lax.rem(g + k, n_outer), i), device_id_type=MESH
        )
        return carry

    lax.fori_loop(1, n_inner, greet_plane, 0)
    lax.fori_loop(1, n_outer, greet_column, 0)

    width = n_inner * 8
    couples = sep_rows.shape[1]
    sel_t = (
        lax.broadcasted_iota(jnp.int32, (width, couples), 0)
        == jnp.broadcast_to(sep_rows[...], (width, couples))
    ).astype(F32)
    y_t = mul(b_t[...], leaf_linv[...], NT)
    contrib_t = mul(y_t, leaf_lower[...], NT)
    update = mul(sel_t, contrib_t, NT)
    a_src[...] = wide(update).reshape(n_inner, 8, 128)
    by_owner(sep_lower_t[...], n_outer, n_inner, sp_src)
    sp_buf[i] = sp_src[i]
    sl_buf[i] = sep_linv[...]
    su_buf[i] = sep_uinv[...]
    l_buf[g] = root_linv[...]
    u_buf[g] = root_uinv[...]

    pl.semaphore_wait(barrier, n_inner + n_outer - 2)

    to_plane(A, lambda peer, k: a_src.at[peer], lambda peer, k: a_rcv.at[k - 1])
    to_plane(SL, lambda peer, k: sep_linv, lambda peer, k: sl_buf.at[i])
    to_plane(SP, lambda peer, k: sp_src.at[peer], lambda peer, k: sp_buf.at[i])
    to_column(L, root_linv, l_buf.at[g])
    to_column(U, root_uinv, u_buf.at[g])

    arrived(A, a_rcv)
    b_buf[i] = wide(b_sep[...]) - (a_src[i] + jnp.sum(a_rcv[...], axis=0))
    to_plane(B, lambda peer, k: b_buf.at[i], lambda peer, k: b_buf.at[i])
    to_plane(SU, lambda peer, k: sep_uinv, lambda peer, k: su_buf.at[i])

    uy_t = mul(y_t, leaf_uinv[...], NT)
    coupling = mul(leaf_uinv[...], mul(leaf_upper[...], sel_t, NT))
    arrived(SL, sl_buf.at[others])
    arrived(SP, sp_buf.at[others])
    to_root = mul(sp_buf[...].reshape(width, 128)[:, :rb], sl_buf[...].reshape(width, width), TN)

    arrived(B, b_buf.at[others])
    rhs_sep = b_buf[...].reshape(width, 128)[:, :64]
    part = mul(to_root, rhs_sep)
    mine = lax.broadcasted_iota(jnp.int32, (rb, 64), 0) // 8 == g
    own = jnp.where(mine, jnp.concatenate([b_root[...]] * n_outer, axis=0), 0.0)
    rz_buf[g] = folded(own - part)
    to_column(RZ, rz_buf.at[g], rz_buf.at[g])
    y_own = mul(sep_linv[...], rhs_sep)
    arrived(RZ, rz_buf.at[others_z])

    def root_gather(phase, buf, block):
        buf[:, i] = block.reshape(n_outer // 2, 8, 128)
        to_plane(phase, lambda peer, k: buf.at[:, i], lambda peer, k: buf.at[:, i])

    def root_value(phase, buf):
        arrived(phase, buf.at[:, others])
        return buf[...].reshape(n_outer // 2 * n_inner * 8, 128)

    root_gather(D, d_buf, jnp.sum(rz_buf[...], axis=0))
    arrived(L, l_buf.at[others_z])
    lower_rows = l_buf[...].reshape(rb, l_buf.shape[2])
    y_root = unfolded_product(lower_rows, root_value(D, d_buf))
    root_gather(E_, e_buf, folded(y_root))

    size = g_blocks.shape[1]
    stored = block_cols.shape[1]
    for r in range(2):
        for c in range(2):
            for blocks, whole in ((g_blocks, hg), (c_blocks, hc)):
                total = jnp.zeros((size, size), F32)
                for w in range(stored):
                    at = (r * stored + w) * size
                    weight = jnp.where(block_cols[r, w] == c, 1.0, 0.0).astype(F32)
                    total = total + weight * blocks[at : at + size, :]
                whole[r * size : (r + 1) * size, c * size : (c + 1) * size] = total
    leaf_count = basis_leaf.shape[0]
    q_all[:leaf_count, :] = basis_leaf[...]
    q_all[leaf_count : leaf_count + 8, :] = basis_sep[...]
    q_all[leaf_count + 8 : leaf_count + 16, :] = basis_root[...]
    arrived(SU, su_buf.at[others])
    from_sep = mul(coupling, su_buf[...].reshape(width, width))

    arrived(U, u_buf.at[others_z])
    upper_rows = u_buf[...].reshape(rb, u_buf.shape[2])
    x_root = unfolded_product(upper_rows, root_value(E_, e_buf))
    root_gather(F_, f_buf, folded(x_root))
    row_ids = lax.broadcasted_iota(jnp.int32, (8, rb), 0)
    col_ids = lax.broadcasted_iota(jnp.int32, (8, rb), 1)
    pick = (col_ids == row_ids + 8 * g).astype(F32)
    x_root_t = mul(x_root, pick, ((0,), (1,)))

    z_own = y_own - unfolded_product(sep_upper[...], root_value(F_, f_buf))
    z_buf[i] = wide(z_own)
    to_plane(Z, lambda peer, k: z_buf.at[i], lambda peer, k: z_buf.at[i])
    arrived(Z, z_buf.at[others])
    z_t = jnp.transpose(z_buf[...].reshape(width, 128))[:64]
    x_leaf_t = uy_t - mul(z_t, from_sep, NT)
    x_sep_t = mul(z_t, sep_uinv[...], NT)
    x_t = jnp.concatenate([x_leaf_t, x_sep_t, x_root_t], axis=1)

    proj_t = mul(x_t, q_all[...])
    per = PIECES_P // n_inner
    for t in range(PIECES_P):
        r, c = t // 4, t % 4
        p_src[t // per, t % per] = proj_t[8 * r : 8 * r + 8, 128 * c : 128 * c + 128]
    to_plane(PR, lambda peer, k: p_src.at[peer], lambda peer, k: p_rcv.at[k - 1])
    arrived(PR, p_rcv)
    pz_buf[g] = p_src[i] + jnp.sum(p_rcv[...], axis=0)
    to_column(PZ, pz_buf.at[g], pz_buf.at[g])
    arrived(PZ, pz_buf.at[others_z])
    pc_buf[i] = jnp.sum(pz_buf[...], axis=0) / nodes
    to_plane(PC, lambda peer, k: pc_buf.at[i], lambda peer, k: pc_buf.at[i])
    arrived(PC, pc_buf.at[others])
    coefs = jnp.concatenate(
        [
            jnp.concatenate(
                [pc_buf[(4 * r + c) // per, (4 * r + c) % per] for c in range(4)], axis=1
            )
            for r in range(8)
        ],
        axis=0,
    )
    coef_t[...] = coefs
    clean_t = x_t - mul(coefs, q_all[...], NT)

    gram_part = mul(clean_t, clean_t, NT)
    clean_leaf_t = clean_t[:, :leaf_count]
    g_part = mul(mul(clean_leaf_t, hg[...]), clean_leaf_t, NT)
    c_part = mul(mul(clean_leaf_t, hc[...]), clean_leaf_t, NT)
    per_k = PIECES_K // n_own
    products = jnp.concatenate(
        [jnp.concatenate([g_part, c_part], axis=1), wide(gram_part)], axis=0
    )
    k_src[...] = products.reshape(n_own, per_k, 8, 128)
    owner = i // stride
    owns = lax.rem(i, stride) == 0

    def to_owner(k, carry):
        peer = lax.rem(i + k, n_inner)

        @pl.when(lax.rem(peer, stride) == 0)
        def _():
            pltpu.make_async_remote_copy(
                src_ref=k_src.at[peer // stride],
                dst_ref=k_rcv.at[k - 1],
                send_sem=send.at[KR],
                recv_sem=recv.at[KR],
                device_id=(g, peer),
                device_id_type=MESH,
            ).start()

        return carry

    lax.fori_loop(1, n_inner, to_owner, 0)

    @pl.when(owns)
    def _():
        arrived(KR, k_rcv)
        kz_buf[g] = k_src[owner] + jnp.sum(k_rcv[...], axis=0)
        to_column(KZ, kz_buf.at[g], kz_buf.at[g])
        arrived(KZ, kz_buf.at[others_z])
        kc_buf[owner] = jnp.sum(kz_buf[...], axis=0) / nodes
        to_plane(KC, lambda peer, k: kc_buf.at[owner], lambda peer, k: kc_buf.at[owner])
        arrived(KC, kc_buf.at[pl.ds(0, n_own - 1)])

    @pl.when(jnp.logical_not(owns))
    def _():
        arrived(KC, kc_buf)

    summed = kc_buf[...].reshape(128, 128)
    inverse = inverse_factor(summed[64:, :64])
    v_t = mul(inverse, clean_t)
    v_leaf_t[...] = v_t[:, :leaf_count]
    ends = jnp.concatenate([v_t[:, leaf_count:], jnp.zeros((64, 112), F32)], axis=1)
    ends = jnp.transpose(ends)
    v_sep[...] = ends[0:8]
    v_root[...] = ends[8:16]
    both = mul(inverse, summed[:64])
    red_g[...] = mul(both[:, :64], inverse, NT)
    red_c[...] = mul(both[:, 64:], inverse, NT)

    sent(A, a_rcv)
    sent(B, b_buf.at[others])
    sent(SL, sl_buf.at[others])
    sent(SU, su_buf.at[others])
    sent(SP, sp_buf.at[others])
    sent(L, l_buf.at[others_z])
    sent(U, u_buf.at[others_z])
    sent(RZ, rz_buf.at[others_z])
    sent(D, d_buf.at[:, others])
    sent(E_, e_buf.at[:, others])
    sent(F_, f_buf.at[:, others])
    sent(Z, z_buf.at[others])
    sent(PR, p_rcv)
    sent(PZ, pz_buf.at[others_z])
    sent(PC, pc_buf.at[others])

    @pl.when(owns)
    def _():
        sent(KR, k_src.at[pl.ds(0, n_own - 1)])
        sent(KZ, kz_buf.at[others_z])
        sent(KC, k_rcv)

    @pl.when(jnp.logical_not(owns))
    def _():
        sent(KR, k_src)


def shards(
    n_outer,
    n_inner,
    b_leaf,
    b_sep,
    b_root,
    leaf_linv,
    leaf_uinv,
    leaf_lower,
    leaf_upper,
    sep_rows,
    sep_linv,
    sep_uinv,
    sep_lower,
    sep_upper,
    root_linv,
    root_uinv,
    basis_leaf,
    basis_sep,
    basis_root,
    g_blocks,
    c_blocks,
    block_cols,
):
    nodes, ports = b_leaf.shape
    basis = basis_leaf.shape[1]
    root = root_linv.shape[1]
    width = n_inner * 8
    half = n_outer // 2
    per = PIECES_P // n_inner
    n_own = min(PIECES_K, n_inner)
    per_k = PIECES_K // n_own
    vmem = pl.BlockSpec(memory_space=pltpu.VMEM)
    smem = pl.BlockSpec(memory_space=pltpu.SMEM)
    scratch = [
        (n_inner, 8, 128),
        (n_inner - 1, 8, 128),
        (n_inner, 8, 128),
        (n_inner, 8, width),
        (n_inner, 8, width),
        (n_inner, 8, 128),
        (n_inner, 8, 128),
        (n_outer, 8, root),
        (n_outer, 8, root),
        (n_outer, n_outer * 4, 128),
        (half, n_inner, 8, 128),
        (half, n_inner, 8, 128),
        (half, n_inner, 8, 128),
        (n_inner, 8, 128),
        (n_inner, per, 8, 128),
        (n_inner - 1, per, 8, 128),
        (n_outer, per, 8, 128),
        (n_inner, per, 8, 128),
        (n_own, per_k, 8, 128),
        (n_inner - 1, per_k, 8, 128),
        (n_outer, per_k, 8, 128),
        (n_own, per_k, 8, 128),
        (nodes + 16, basis),
        (nodes, nodes),
        (nodes, nodes),
    ]
    outs = [(ports, nodes), (8, ports), (8, ports), (ports, basis), (ports, ports), (ports, ports)]
    v_leaf_t, v_sep, v_root, coef_t, red_g, red_c = pl.pallas_call(
        functools.partial(kernel, n_outer, n_inner),
        out_shape=[jax.ShapeDtypeStruct(s, F32) for s in outs],
        in_specs=[vmem] * 19 + [smem],
        out_specs=[vmem] * 6,
        scratch_shapes=[pltpu.VMEM(s, F32) for s in scratch]
        + [pltpu.SemaphoreType.DMA((18,)), pltpu.SemaphoreType.DMA((18,))],
        compiler_params=pltpu.CompilerParams(
            collective_id=0, has_side_effects=True, vmem_limit_bytes=48 * 2**20
        ),
    )(
        b_leaf.T,
        b_sep,
        b_root,
        leaf_linv,
        leaf_uinv,
        leaf_lower,
        leaf_upper,
        sep_rows,
        sep_linv,
        sep_uinv,
        sep_lower.T,
        sep_upper,
        root_linv,
        root_uinv,
        basis_leaf,
        basis_sep,
        basis_root,
        g_blocks,
        c_blocks,
        block_cols,
    )
    return v_leaf_t.T, v_sep, v_root, coef_t.T, red_g, red_c


def solution(mesh):
    rows = P(("outer", "inner"), None)
    return jax.shard_map(
        functools.partial(shards, mesh.shape["outer"], mesh.shape["inner"]),
        mesh=mesh,
        in_specs=(rows,) * 10 + (P(None, ("outer", "inner")),) + (rows,) * 9,
        out_specs=(rows, rows, rows, P(), P(), P()),
        check_vma=False,
    )
```

time: 1060 us -> 137 us (0.13)
  waiting for transfers between devices: 602 us -> 0 us
  blocking collectives: 405 us -> 0 us
  Pallas kernels: 0 us -> 116 us
  other arithmetic: 14.4 us -> 0 us
  between operations: 14.7 us -> 0.69 us
  matrix products: 14 us -> 0 us
  local copies, waits for them, and re-layouts: 6.93 us -> 19.7 us
    unnamed x5 -> x0, waiting for transfers between devices: 365 us -> none
    all_gather x6 -> x0, blocking collectives: 256 us -> none  [the longest x1 63.2 us: shards(): lax.all_gather(b_root - t_root, ('outer', 'inner'), axis=0, tiled=True)]
    psum x1 -> x0, waiting for transfers between devices: 238 us -> none  [shards(): coefficients = lax.psum(projected, ('outer', 'inner')) / node_count]
    psum x2 -> x0, blocking collectives: 149 us -> none  [the longest x1 76 us: shards(): gram_matrix = lax.psum(local_gram, ('outer', 'inner')) / node_count]
    pallas_call x0 -> x1, Pallas kernels: none -> 116 us  [shards(): pl.pallas_call(functools.partial(kernel, n_outer, n_inner), out_shape=[ja...]
    unnamed x45 -> x46, local copies, waits for them, and re-layouts: 4.86 us -> 19.7 us
    dot_general x28 -> x0, matrix products: 13.7 us -> none  [the longest x17 8.54 us: matmul_exact(): jnp.dot(left, right, precision=lax.Precision.HIGHEST, preferred_element_t...]
    another operation x5 -> x0, other arithmetic: 12.1 us -> none  [the longest x3 6.52 us: shards(): chol_lower = jnp.linalg.cholesky(gram_matrix)]
  transfers between devices with their start and end apart: 3 -> 0, of which waited for: 3 -> 0; matrix products, arithmetic and copies ran while one was open for 0% -> 0% of each run, Pallas kernels for 0% -> 0%
where the time goes in v1:
time: 137 us; the launch traced here: 136 us
  Pallas kernels  116 us (85%)
  local copies, waits for them, and re-layouts  19.7 us (14%)
    pallas_call x1, Pallas kernels, shards(): pl.pallas_call(functools.partial(kernel, n_outer, n_inner), out_shape=[ja...  116 us
    unnamed x46, local copies, waits for them, and re-layouts  19.7 us

profile of v1, /device:TPU:1, one launch (start us, length us, event | category | flops | bytes accessed | tf_op | source)
XLA Modules:
  0.0 135.9 jit_solution(9586737556765771009)
XLA Ops:
  0.7 0.7 copy-done.19
  1.3 1.0 copy-done
  2.4 1.0 copy-done.1
  3.4 1.0 copy-done.2
  4.5 0.9 copy-done.3
  5.4 0.9 copy-done.4
  6.4 0.9 copy-done.5
  7.3 0.9 copy-done.6
  8.3 0.8 copy-done.7
  9.1 0.8 copy-done.8
  9.9 0.8 copy-done.9
  10.8 0.8 copy-done.10
  11.6 0.8 copy-done.11
  12.5 0.7 copy-done.12
  13.2 0.7 copy-done.13
  13.9 0.7 copy-done.14
  14.6 0.7 copy-done.15
  15.3 0.7 copy-done.16
  16.0 0.7 copy-done.17
  16.7 115.5 %shard_map.235 = (f32[64,256]{1,0:T(8,128)S(1)}, f32[8,64]{1,0:T(8,128)S(1)}, f32[8,64]{1,0:T(8,128)S(1)}, f32[64,512]{1,0:T(8,128)S(1)}, f32[64,64]{1,0:T(8,128)S(1)}, /*index=5*/f32[64,64]{1,0:T(8,128)S(1)}) custom-call(f32[64,256]{1,0:T(8,128)S(1)} %bitcast.5, f32[8,64]{1,0:T(8,128)S(1)} %copy-done.16, f32[8,64]{1,0:T(8,128)S(1)} %copy-done.17, ...), custom_call_target="tpu_custom_call" | custom-call | tf_op jit(solution)/shard_map/pallas_call | solution.py:480
  132.2 0.6 copy.32
  134.0 0.7 copy.35
  134.7 0.6 copy.36
  135.3 0.6 copy.37
  (23 shorter events, 1.2 us)
Async XLA Ops:
  0.6 0.7 copy-start.19
  0.7 0.7 copy-start.18
  1.3 1.0 copy-start
  2.4 1.0 copy-start.1
  3.4 1.0 copy-start.2
  4.5 0.9 copy-start.3
  5.4 0.9 copy-start.4
  6.4 0.9 copy-start.5
  7.3 0.9 copy-start.6
  8.3 0.8 copy-start.7
  9.1 0.8 copy-start.8
  9.9 0.8 copy-start.9
  10.8 0.8 copy-start.10
  11.6 0.8 copy-start.11
  12.5 0.7 copy-start.12
  13.2 0.7 copy-start.13
  13.9 0.7 copy-start.14
  14.6 0.7 copy-start.15
  15.3 0.7 copy-start.16
  16.0 0.7 copy-start.17

commit v2 on v1

--- a/solution.py
+++ b/solution.py
@@ -93,26 +93,26 @@
 def kernel(
     n_outer,
     n_inner,
-    b_t,
-    b_sep,
-    b_root,
-    leaf_linv,
-    leaf_uinv,
-    leaf_lower,
-    leaf_upper,
-    sep_rows,
-    sep_linv,
-    sep_uinv,
-    sep_lower_t,
-    sep_upper,
-    root_linv,
-    root_uinv,
-    basis_leaf,
-    basis_sep,
-    basis_root,
-    g_blocks,
-    c_blocks,
-    block_cols,
+    h_b_t,
+    h_b_sep,
+    h_b_root,
+    h_leaf_linv,
+    h_leaf_uinv,
+    h_leaf_lower,
+    h_leaf_upper,
+    h_sep_rows,
+    h_sep_linv,
+    h_sep_uinv,
+    h_sep_lower_t,
+    h_sep_upper,
+    h_root_linv,
+    h_root_uinv,
+    h_basis_leaf,
+    h_basis_sep,
+    h_basis_root,
+    h_g_blocks,
+    h_c_blocks,
+    h_block_cols,
     v_leaf_t,
     v_sep,
     v_root,
@@ -144,15 +144,30 @@
     q_all,
     hg,
     hc,
+    b_t,
+    b_sep,
+    b_root,
+    leaf_linv,
+    leaf_uinv,
+    leaf_lower,
+    leaf_upper,
+    sep_rows,
+    sep_lower_t,
+    sep_upper,
+    g_blocks,
+    c_blocks,
+    block_cols,
     send,
     recv,
+    here,
 ):
     g = lax.axis_index("outer")
     i = lax.axis_index("inner")
     rb = n_outer * 8
     n_own = kc_buf.shape[0]
     stride = n_inner // n_own
-    nodes = float(n_outer * n_inner * (basis_leaf.shape[0] + 16))
+    leaf_count = h_basis_leaf.shape[0]
+    nodes = float(n_outer * n_inner * (leaf_count + 16))
     A, B, SL, SU, SP, L, U, RZ, D, E_, F_, Z, PR, PZ, PC, KR, KZ, KC = range(18)
 
     def to_plane(phase, src, dst):
@@ -194,6 +209,39 @@
     others = pl.ds(0, n_inner - 1)
     others_z = pl.ds(0, n_outer - 1)
 
+    own_slots = {
+        "b_t": (h_b_t, b_t),
+        "leaf_linv": (h_leaf_linv, leaf_linv),
+        "leaf_lower": (h_leaf_lower, leaf_lower),
+        "sep_rows": (h_sep_rows, sep_rows),
+        "sep_lower_t": (h_sep_lower_t, sep_lower_t),
+        "sep_linv": (h_sep_linv, sl_buf.at[i]),
+        "root_linv": (h_root_linv, l_buf.at[g]),
+        "root_uinv": (h_root_uinv, u_buf.at[g]),
+        "sep_uinv": (h_sep_uinv, su_buf.at[i]),
+        "b_sep": (h_b_sep, b_sep),
+        "leaf_uinv": (h_leaf_uinv, leaf_uinv),
+        "leaf_upper": (h_leaf_upper, leaf_upper),
+        "b_root": (h_b_root, b_root),
+        "sep_upper": (h_sep_upper, sep_upper),
+        "g_blocks": (h_g_blocks, g_blocks),
+        "c_blocks": (h_c_blocks, c_blocks),
+        "block_cols": (h_block_cols, block_cols),
+        "basis_leaf": (h_basis_leaf, q_all.at[pl.ds(0, leaf_count)]),
+        "basis_sep": (h_basis_sep, q_all.at[pl.ds(leaf_count, 8)]),
+        "basis_root": (h_basis_root, q_all.at[pl.ds(leaf_count + 8, 8)]),
+    }
+    loads = {
+        name: pltpu.make_async_copy(src, dst, here.at[n])
+        for n, (name, (src, dst)) in enumerate(own_slots.items())
+    }
+    for load in loads.values():
+        load.start()
+
+    def loaded(*names):
+        for name in names:
+            loads[name].wait()
+
     barrier = pltpu.get_barrier_semaphore()
 
     def greet_plane(k, carry):
@@ -211,6 +259,7 @@
     lax.fori_loop(1, n_inner, greet_plane, 0)
     lax.fori_loop(1, n_outer, greet_column, 0)
 
+    loaded("b_t", "leaf_linv", "leaf_lower", "sep_rows", "sep_lower_t")
     width = n_inner * 8
     couples = sep_rows.shape[1]
     sel_t = (
@@ -223,24 +272,20 @@
     a_src[...] = wide(update).reshape(n_inner, 8, 128)
     by_owner(sep_lower_t[...], n_outer, n_inner, sp_src)
     sp_buf[i] = sp_src[i]
-    sl_buf[i] = sep_linv[...]
-    su_buf[i] = sep_uinv[...]
-    l_buf[g] = root_linv[...]
-    u_buf[g] = root_uinv[...]
+    loaded("sep_linv", "root_linv", "root_uinv", "sep_uinv", "b_sep")
 
     pl.semaphore_wait(barrier, n_inner + n_outer - 2)
 
     to_plane(A, lambda peer, k: a_src.at[peer], lambda peer, k: a_rcv.at[k - 1])
-    to_plane(SL, lambda peer, k: sep_linv, lambda peer, k: sl_buf.at[i])
+    to_plane(SL, lambda peer, k: sl_buf.at[i], lambda peer, k: sl_buf.at[i])
     to_plane(SP, lambda peer, k: sp_src.at[peer], lambda peer, k: sp_buf.at[i])
-    to_column(L, root_linv, l_buf.at[g])
-    to_column(U, root_uinv, u_buf.at[g])
+    to_column(L, l_buf.at[g], l_buf.at[g])
 
     arrived(A, a_rcv)
     b_buf[i] = wide(b_sep[...]) - (a_src[i] + jnp.sum(a_rcv[...], axis=0))
     to_plane(B, lambda peer, k: b_buf.at[i], lambda peer, k: b_buf.at[i])
-    to_plane(SU, lambda peer, k: sep_uinv, lambda peer, k: su_buf.at[i])
-
+
+    loaded("leaf_uinv", "leaf_upper", "b_root")
     uy_t = mul(y_t, leaf_uinv[...], NT)
     coupling = mul(leaf_uinv[...], mul(leaf_upper[...], sel_t, NT))
     arrived(SL, sl_buf.at[others])
@@ -254,7 +299,8 @@
     own = jnp.where(mine, jnp.concatenate([b_root[...]] * n_outer, axis=0), 0.0)
     rz_buf[g] = folded(own - part)
     to_column(RZ, rz_buf.at[g], rz_buf.at[g])
-    y_own = mul(sep_linv[...], rhs_sep)
+    to_plane(SU, lambda peer, k: su_buf.at[i], lambda peer, k: su_buf.at[i])
+    y_own = mul(sl_buf[i], rhs_sep)
     arrived(RZ, rz_buf.at[others_z])
 
     def root_gather(phase, buf, block):
@@ -266,11 +312,13 @@
         return buf[...].reshape(n_outer // 2 * n_inner * 8, 128)
 
     root_gather(D, d_buf, jnp.sum(rz_buf[...], axis=0))
+    to_column(U, u_buf.at[g], u_buf.at[g])
     arrived(L, l_buf.at[others_z])
     lower_rows = l_buf[...].reshape(rb, l_buf.shape[2])
     y_root = unfolded_product(lower_rows, root_value(D, d_buf))
     root_gather(E_, e_buf, folded(y_root))
 
+    loaded("g_blocks", "c_blocks", "block_cols", "basis_leaf", "basis_sep", "basis_root", "sep_upper")
     size = g_blocks.shape[1]
     stored = block_cols.shape[1]
     for r in range(2):
@@ -279,13 +327,9 @@
                 total = jnp.zeros((size, size), F32)
                 for w in range(stored):
                     at = (r * stored + w) * size
-                    weight = jnp.where(block_cols[r, w] == c, 1.0, 0.0).astype(F32)
+                    weight = (block_cols[r : r + 1, w : w + 1] == c).astype(F32)
                     total = total + weight * blocks[at : at + size, :]
                 whole[r * size : (r + 1) * size, c * size : (c + 1) * size] = total
-    leaf_count = basis_leaf.shape[0]
-    q_all[:leaf_count, :] = basis_leaf[...]
-    q_all[leaf_count : leaf_count + 8, :] = basis_sep[...]
-    q_all[leaf_count + 8 : leaf_count + 16, :] = basis_root[...]
     arrived(SU, su_buf.at[others])
     from_sep = mul(coupling, su_buf[...].reshape(width, width))
 
@@ -304,7 +348,7 @@
     arrived(Z, z_buf.at[others])
     z_t = jnp.transpose(z_buf[...].reshape(width, 128))[:64]
     x_leaf_t = uy_t - mul(z_t, from_sep, NT)
-    x_sep_t = mul(z_t, sep_uinv[...], NT)
+    x_sep_t = mul(z_t, su_buf[i], NT)
     x_t = jnp.concatenate([x_leaf_t, x_sep_t, x_root_t], axis=1)
 
     proj_t = mul(x_t, q_all[...])
@@ -448,7 +492,7 @@
     n_own = min(PIECES_K, n_inner)
     per_k = PIECES_K // n_own
     vmem = pl.BlockSpec(memory_space=pltpu.VMEM)
-    smem = pl.BlockSpec(memory_space=pltpu.SMEM)
+    hbm = pl.BlockSpec(memory_space=pltpu.HBM)
     scratch = [
         (n_inner, 8, 128),
         (n_inner - 1, 8, 128),
@@ -476,19 +520,36 @@
         (nodes, nodes),
         (nodes, nodes),
     ]
+    b_leaf_t, sep_lower_t = b_leaf.T, sep_lower.T
+    kept = (
+        b_leaf_t,
+        b_sep,
+        b_root,
+        leaf_linv,
+        leaf_uinv,
+        leaf_lower,
+        leaf_upper,
+        sep_rows,
+        sep_lower_t,
+        sep_upper,
+        g_blocks,
+        c_blocks,
+        block_cols,
+    )
     outs = [(ports, nodes), (8, ports), (8, ports), (ports, basis), (ports, ports), (ports, ports)]
     v_leaf_t, v_sep, v_root, coef_t, red_g, red_c = pl.pallas_call(
         functools.partial(kernel, n_outer, n_inner),
         out_shape=[jax.ShapeDtypeStruct(s, F32) for s in outs],
-        in_specs=[vmem] * 19 + [smem],
+        in_specs=[hbm] * 20,
         out_specs=[vmem] * 6,
         scratch_shapes=[pltpu.VMEM(s, F32) for s in scratch]
-        + [pltpu.SemaphoreType.DMA((18,)), pltpu.SemaphoreType.DMA((18,))],
+        + [pltpu.VMEM(x.shape, x.dtype) for x in kept]
+        + [pltpu.SemaphoreType.DMA((n,)) for n in (18, 18, 20)],
         compiler_params=pltpu.CompilerParams(
-            collective_id=0, has_side_effects=True, vmem_limit_bytes=48 * 2**20
+            collective_id=0, has_side_effects=True, vmem_limit_bytes=64 * 2**20
         ),
     )(
-        b_leaf.T,
+        b_leaf_t,
         b_sep,
         b_root,
         leaf_linv,
@@ -498,7 +559,7 @@
         sep_rows,
         sep_linv,
         sep_uinv,
-        sep_lower.T,
+        sep_lower_t,
         sep_upper,
         root_linv,
         root_uinv,

time: 137 us -> 112 us (0.82)
  local copies, waits for them, and re-layouts: 19.7 us -> 4.93 us
  Pallas kernels: 116 us -> 106 us
    unnamed x46 -> x16, local copies, waits for them, and re-layouts: 19.7 us -> 4.93 us
    pallas_call x1, Pallas kernels: 116 us -> 106 us  [shards(): pl.pallas_call(functools.partial(kernel, n_outer, n_inner), out_shape=[ja...]
where the time goes in v2:
time: 112 us; the launch traced here: 111 us
  Pallas kernels  106 us (95%)
  local copies, waits for them, and re-layouts  4.93 us (4%)
    pallas_call x1, Pallas kernels, shards(): pl.pallas_call(functools.partial(kernel, n_outer, n_inner), out_shape=[ja...  106 us
    unnamed x16, local copies, waits for them, and re-layouts  4.93 us

profile of v2, /device:TPU:1, one launch (start us, length us, event | category | flops | bytes accessed | tf_op | source)
XLA Modules:
  0.0 111.2 jit_solution(1082852380409663536)
XLA Ops:
  0.6 105.6 %shard_map.235 = (f32[64,256]{1,0:T(8,128)}, f32[8,64]{1,0:T(8,128)}, f32[8,64]{1,0:T(8,128)}, f32[64,512]{1,0:T(8,128)}, f32[64,64]{1,0:T(8,128)}, /*index=5*/f32[64,64]{1,0:T(8,128)}) custom-call(f32[64,256]{1,0:T(8,128)} %bitcast.5, f32[8,64]{1,0:T(8,128)} %h_b_sep.1, f32[8,64]{1,0:T(8,128)} %h_b_root.1, f32[256,256]{1,0:T(8,128)} %h_leaf_linv.1, ...), custom_call_target="tpu_custom_call" | custom-call | tf_op jit(solution)/shard_map/pallas_call | solution.py:540
  106.3 0.0 copy-start
  106.3 0.0 copy-start.4
  106.3 1.5 %copy.32 = f32[256,64]{0,1:T(8,128)} copy(f32[256,64]{0,1:T(8,128)} %bitcast.7) | data formatting | bytes 131072
  107.8 0.0 copy-done.4
  107.8 0.0 copy-start.3
  107.8 0.6 copy.33
  108.4 0.1 copy-done.3
  108.5 0.6 copy.34
  109.1 0.0 copy-done
  109.1 0.0 copy-start.2
  109.1 0.7 copy.35
  109.7 0.1 copy-done.2
  109.8 0.0 copy-start.1
  109.8 0.6 copy.36
  110.5 0.2 copy-done.1
  110.6 0.6 copy.37
Async XLA Ops:
  106.3 2.8 %copy-start = (f32[64,512]{1,0:T(8,128)S(1)}, f32[64,512]{1,0:T(8,128)}, u32[]{:S(2)}) copy-start(f32[64,512]{1,0:T(8,128)} %get-tuple-element.15) | copy-start | bytes 393220
  106.3 1.5 %copy-start.4 = (f32[8,64]{1,0:T(8,128)S(1)}, f32[8,64]{1,0:T(8,128)}, u32[]{:S(2)}) copy-start(f32[8,64]{1,0:T(8,128)} %get-tuple-element.25) | copy-start | bytes 6148
  107.8 0.7 copy-start.3
  109.1 0.8 copy-start.2
  109.8 0.8 copy-start.1

commit v3 on v2

--- a/solution.py
+++ b/solution.py
@@ -126,17 +126,25 @@
     su_buf,
     sp_src,
     sp_buf,
+    ss_src,
+    ss_buf,
     l_buf,
     u_buf,
     rz_buf,
     d_buf,
     e_buf,
-    f_buf,
-    z_buf,
+    n_src,
+    n_rcv,
+    n_buf,
+    m_src,
+    m_rcv,
+    m_buf,
     p_src,
     p_rcv,
     pz_buf,
-    pc_buf,
+    w_src,
+    w_rcv,
+    w_buf,
     k_src,
     k_rcv,
     kz_buf,
@@ -168,7 +176,7 @@
     stride = n_inner // n_own
     leaf_count = h_basis_leaf.shape[0]
     nodes = float(n_outer * n_inner * (leaf_count + 16))
-    A, B, SL, SU, SP, L, U, RZ, D, E_, F_, Z, PR, PZ, PC, KR, KZ, KC = range(18)
+    A, B, SL, SU, SP, SS, L, U, RZ, D, E_, N1, N2, N3, N4, P1, P2, W1, W2, KR, KZ, KG, KC = range(23)
 
     def to_plane(phase, src, dst):
         def one(k, carry):
@@ -189,7 +197,7 @@
         def one(k, carry):
             peer = lax.rem(g + k, n_outer)
             pltpu.make_async_remote_copy(
-                src_ref=src,
+                src_ref=src(peer),
                 dst_ref=dst,
                 send_sem=send.at[phase],
                 recv_sem=recv.at[phase],
@@ -259,7 +267,7 @@
     lax.fori_loop(1, n_inner, greet_plane, 0)
     lax.fori_loop(1, n_outer, greet_column, 0)
 
-    loaded("b_t", "leaf_linv", "leaf_lower", "sep_rows", "sep_lower_t")
+    loaded("b_t", "leaf_linv", "leaf_lower", "sep_rows")
     width = n_inner * 8
     couples = sep_rows.shape[1]
     sel_t = (
@@ -270,8 +278,11 @@
     contrib_t = mul(y_t, leaf_lower[...], NT)
     update = mul(sel_t, contrib_t, NT)
     a_src[...] = wide(update).reshape(n_inner, 8, 128)
+    loaded("sep_lower_t", "sep_upper")
     by_owner(sep_lower_t[...], n_outer, n_inner, sp_src)
     sp_buf[i] = sp_src[i]
+    by_owner(sep_upper[...], n_outer, n_inner, ss_src)
+    ss_buf[i] = ss_src[i]
     loaded("sep_linv", "root_linv", "root_uinv", "sep_uinv", "b_sep")
 
     pl.semaphore_wait(barrier, n_inner + n_outer - 2)
@@ -279,29 +290,37 @@
     to_plane(A, lambda peer, k: a_src.at[peer], lambda peer, k: a_rcv.at[k - 1])
     to_plane(SL, lambda peer, k: sl_buf.at[i], lambda peer, k: sl_buf.at[i])
     to_plane(SP, lambda peer, k: sp_src.at[peer], lambda peer, k: sp_buf.at[i])
-    to_column(L, l_buf.at[g], l_buf.at[g])
+    to_column(L, lambda peer: l_buf.at[g], l_buf.at[g])
+
+    loaded("leaf_uinv", "leaf_upper", "b_root", "basis_leaf", "basis_sep", "basis_root")
+    uy_t = mul(y_t, leaf_uinv[...], NT)
+    coupling = mul(leaf_uinv[...], mul(leaf_upper[...], sel_t, NT))
+    n_src[...] = mul(coupling, q_all[:leaf_count, :], TN).reshape(n_src.shape)
 
     arrived(A, a_rcv)
     b_buf[i] = wide(b_sep[...]) - (a_src[i] + jnp.sum(a_rcv[...], axis=0))
     to_plane(B, lambda peer, k: b_buf.at[i], lambda peer, k: b_buf.at[i])
-
-    loaded("leaf_uinv", "leaf_upper", "b_root")
-    uy_t = mul(y_t, leaf_uinv[...], NT)
-    coupling = mul(leaf_uinv[...], mul(leaf_upper[...], sel_t, NT))
+    to_plane(N1, lambda peer, k: n_src.at[peer], lambda peer, k: n_rcv.at[k - 1])
+    to_plane(SU, lambda peer, k: su_buf.at[i], lambda peer, k: su_buf.at[i])
+    to_plane(SS, lambda peer, k: ss_src.at[peer], lambda peer, k: ss_buf.at[i])
+
     arrived(SL, sl_buf.at[others])
     arrived(SP, sp_buf.at[others])
-    to_root = mul(sp_buf[...].reshape(width, 128)[:, :rb], sl_buf[...].reshape(width, width), TN)
+    sep_inverse = sl_buf[...].reshape(width, width)
+    to_root = mul(sp_buf[...].reshape(width, 128)[:, :rb], sep_inverse, TN)
 
     arrived(B, b_buf.at[others])
-    rhs_sep = b_buf[...].reshape(width, 128)[:, :64]
-    part = mul(to_root, rhs_sep)
+    rhs_sep = b_buf[...].reshape(width, 128)
+    part = mul(to_root, rhs_sep[:, :64])
     mine = lax.broadcasted_iota(jnp.int32, (rb, 64), 0) // 8 == g
     own = jnp.where(mine, jnp.concatenate([b_root[...]] * n_outer, axis=0), 0.0)
     rz_buf[g] = folded(own - part)
-    to_column(RZ, rz_buf.at[g], rz_buf.at[g])
-    to_plane(SU, lambda peer, k: su_buf.at[i], lambda peer, k: su_buf.at[i])
-    y_own = mul(sl_buf[i], rhs_sep)
-    arrived(RZ, rz_buf.at[others_z])
+    to_column(RZ, lambda peer: rz_buf.at[g], rz_buf.at[g])
+    to_column(U, lambda peer: u_buf.at[g], u_buf.at[g])
+
+    arrived(N1, n_rcv)
+    n_buf[i] = q_all[leaf_count : leaf_count + 8, :] - (n_src[i] + jnp.sum(n_rcv[...], axis=0))
+    to_plane(N2, lambda peer, k: n_buf.at[i], lambda peer, k: n_buf.at[i])
 
     def root_gather(phase, buf, block):
         buf[:, i] = block.reshape(n_outer // 2, 8, 128)
@@ -311,14 +330,43 @@
         arrived(phase, buf.at[:, others])
         return buf[...].reshape(n_outer // 2 * n_inner * 8, 128)
 
+    arrived(RZ, rz_buf.at[others_z])
     root_gather(D, d_buf, jnp.sum(rz_buf[...], axis=0))
-    to_column(U, u_buf.at[g], u_buf.at[g])
+
+    y_own = mul(sl_buf[i], rhs_sep[:, :64])
+    sep_y_t = mul(jnp.transpose(rhs_sep)[:64], sep_inverse, NT)
+    arrived(SU, su_buf.at[others])
+    sep_upper_inverse = su_buf[...].reshape(width, width)
+    from_sep = mul(coupling, sep_upper_inverse)
+    start_t = jnp.concatenate(
+        [uy_t - mul(sep_y_t, from_sep, NT), mul(sep_y_t, su_buf[i], NT)], axis=1
+    )
+    proj_t = mul(start_t, q_all[: leaf_count + 8, :])
+    per = PIECES_P // n_inner
+    for t in range(PIECES_P):
+        r, c = t // 4, t % 4
+        p_src[t // per, t % per] = proj_t[8 * r : 8 * r + 8, 128 * c : 128 * c + 128]
+    to_plane(P1, lambda peer, k: p_src.at[peer], lambda peer, k: p_rcv.at[k - 1])
+
+    arrived(SS, ss_buf.at[others])
+    sep_by_root = ss_buf[...].reshape(width, 128)[:, :rb]
+    arrived(N2, n_buf.at[others])
+    m_src[...] = mul(
+        mul(sep_upper_inverse, sep_by_root), n_buf[...].reshape(width, n_buf.shape[2]), TN
+    ).reshape(m_src.shape)
+    m_rcv[g] = m_src[g]
+    to_column(N3, lambda peer: m_src.at[peer], m_rcv.at[g])
+
     arrived(L, l_buf.at[others_z])
     lower_rows = l_buf[...].reshape(rb, l_buf.shape[2])
     y_root = unfolded_product(lower_rows, root_value(D, d_buf))
     root_gather(E_, e_buf, folded(y_root))
 
-    loaded("g_blocks", "c_blocks", "block_cols", "basis_leaf", "basis_sep", "basis_root", "sep_upper")
+    arrived(P1, p_rcv)
+    pz_buf[g] = p_src[i] + jnp.sum(p_rcv[...], axis=0)
+    to_column(P2, lambda peer: pz_buf.at[g], pz_buf.at[g])
+
+    loaded("g_blocks", "c_blocks", "block_cols")
     size = g_blocks.shape[1]
     stored = block_cols.shape[1]
     for r in range(2):
@@ -330,105 +378,125 @@
                     weight = (block_cols[r : r + 1, w : w + 1] == c).astype(F32)
                     total = total + weight * blocks[at : at + size, :]
                 whole[r * size : (r + 1) * size, c * size : (c + 1) * size] = total
-    arrived(SU, su_buf.at[others])
-    from_sep = mul(coupling, su_buf[...].reshape(width, width))
+
+    arrived(N3, m_rcv.at[others_z])
+    m_buf[g] = jnp.sum(m_rcv[...], axis=0) - q_all[leaf_count + 8 : leaf_count + 16, :]
+    to_column(N4, lambda peer: m_buf.at[g], m_buf.at[g])
+    arrived(P2, pz_buf.at[others_z])
+    proj_start = jnp.sum(pz_buf[...], axis=0)
 
     arrived(U, u_buf.at[others_z])
     upper_rows = u_buf[...].reshape(rb, u_buf.shape[2])
     x_root = unfolded_product(upper_rows, root_value(E_, e_buf))
-    root_gather(F_, f_buf, folded(x_root))
+
+    sep_part = wide(mul(sep_by_root, x_root)).reshape(n_inner, 8, 128)
+    arrived(N4, m_buf.at[others_z])
+    proj_t = mul(x_root, m_buf[...].reshape(rb, m_buf.shape[2]), TN)
+    w_src[:, 0] = sep_part
+    for t in range(PIECES_P):
+        r, c = t // 4, t % 4
+        w_src[t // per, 1 + t % per] = proj_t[8 * r : 8 * r + 8, 128 * c : 128 * c + 128]
+    to_plane(W1, lambda peer, k: w_src.at[peer], lambda peer, k: w_rcv.at[k - 1])
     row_ids = lax.broadcasted_iota(jnp.int32, (8, rb), 0)
     col_ids = lax.broadcasted_iota(jnp.int32, (8, rb), 1)
     pick = (col_ids == row_ids + 8 * g).astype(F32)
     x_root_t = mul(x_root, pick, ((0,), (1,)))
-
-    z_own = y_own - unfolded_product(sep_upper[...], root_value(F_, f_buf))
-    z_buf[i] = wide(z_own)
-    to_plane(Z, lambda peer, k: z_buf.at[i], lambda peer, k: z_buf.at[i])
-    arrived(Z, z_buf.at[others])
-    z_t = jnp.transpose(z_buf[...].reshape(width, 128))[:64]
+    arrived(W1, w_rcv)
+    moved = w_src[i] + jnp.sum(w_rcv[...], axis=0)
+    w_buf[i, 0] = wide(y_own) - moved[0]
+    w_buf[i, pl.ds(1, per)] = (proj_start - moved[1:]) / nodes
+    to_plane(W2, lambda peer, k: w_buf.at[i], lambda peer, k: w_buf.at[i])
+    arrived(W2, w_buf.at[others])
+
+    z_t = jnp.transpose(w_buf[:, 0].reshape(width, 128))[:64]
     x_leaf_t = uy_t - mul(z_t, from_sep, NT)
     x_sep_t = mul(z_t, su_buf[i], NT)
     x_t = jnp.concatenate([x_leaf_t, x_sep_t, x_root_t], axis=1)
-
-    proj_t = mul(x_t, q_all[...])
-    per = PIECES_P // n_inner
-    for t in range(PIECES_P):
-        r, c = t // 4, t % 4
-        p_src[t // per, t % per] = proj_t[8 * r : 8 * r + 8, 128 * c : 128 * c + 128]
-    to_plane(PR, lambda peer, k: p_src.at[peer], lambda peer, k: p_rcv.at[k - 1])
-    arrived(PR, p_rcv)
-    pz_buf[g] = p_src[i] + jnp.sum(p_rcv[...], axis=0)
-    to_column(PZ, pz_buf.at[g], pz_buf.at[g])
-    arrived(PZ, pz_buf.at[others_z])
-    pc_buf[i] = jnp.sum(pz_buf[...], axis=0) / nodes
-    to_plane(PC, lambda peer, k: pc_buf.at[i], lambda peer, k: pc_buf.at[i])
-    arrived(PC, pc_buf.at[others])
     coefs = jnp.concatenate(
         [
             jnp.concatenate(
-                [pc_buf[(4 * r + c) // per, (4 * r + c) % per] for c in range(4)], axis=1
+                [w_buf[(4 * r + c) // per, 1 + (4 * r + c) % per] for c in range(4)], axis=1
             )
             for r in range(8)
         ],
         axis=0,
     )
+    clean_t = x_t - mul(coefs, q_all[...], NT)
+
+    per_k = PIECES_K // n_own
+    half = n_own // 2
+    owner = i // stride
+    owns = lax.rem(i, stride) == 0
+    owns_gram = jnp.logical_and(owns, owner >= half)
+    owns_rest = jnp.logical_and(owns, owner < half)
+
+    def to_owners(first):
+        def one(k, carry):
+            peer = lax.rem(i + k, n_inner)
+            at = peer // stride
+
+            @pl.when(jnp.logical_and(lax.rem(peer, stride) == 0, at // half == first // half))
+            def _():
+                pltpu.make_async_remote_copy(
+                    src_ref=k_src.at[at],
+                    dst_ref=k_rcv.at[k - 1],
+                    send_sem=send.at[KR],
+                    recv_sem=recv.at[KR],
+                    device_id=(g, peer),
+                    device_id_type=MESH,
+                ).start()
+
+            return carry
+
+        lax.fori_loop(1, n_inner, one, 0)
+
+    k_src[half:] = wide(mul(clean_t, clean_t, NT)).reshape(half, per_k, 8, 128)
+    to_owners(half)
+    clean_leaf_t = clean_t[:, :leaf_count]
     coef_t[...] = coefs
-    clean_t = x_t - mul(coefs, q_all[...], NT)
-
-    gram_part = mul(clean_t, clean_t, NT)
-    clean_leaf_t = clean_t[:, :leaf_count]
     g_part = mul(mul(clean_leaf_t, hg[...]), clean_leaf_t, NT)
     c_part = mul(mul(clean_leaf_t, hc[...]), clean_leaf_t, NT)
-    per_k = PIECES_K // n_own
-    products = jnp.concatenate(
-        [jnp.concatenate([g_part, c_part], axis=1), wide(gram_part)], axis=0
-    )
-    k_src[...] = products.reshape(n_own, per_k, 8, 128)
-    owner = i // stride
-    owns = lax.rem(i, stride) == 0
-
-    def to_owner(k, carry):
-        peer = lax.rem(i + k, n_inner)
-
-        @pl.when(lax.rem(peer, stride) == 0)
-        def _():
-            pltpu.make_async_remote_copy(
-                src_ref=k_src.at[peer // stride],
-                dst_ref=k_rcv.at[k - 1],
-                send_sem=send.at[KR],
-                recv_sem=recv.at[KR],
-                device_id=(g, peer),
-                device_id_type=MESH,
-            ).start()
-
-        return carry
-
-    lax.fori_loop(1, n_inner, to_owner, 0)
+    k_src[:half] = jnp.concatenate([g_part, c_part], axis=1).reshape(half, per_k, 8, 128)
+    to_owners(0)
 
     @pl.when(owns)
     def _():
         arrived(KR, k_rcv)
         kz_buf[g] = k_src[owner] + jnp.sum(k_rcv[...], axis=0)
-        to_column(KZ, kz_buf.at[g], kz_buf.at[g])
+        to_column(KZ, lambda peer: kz_buf.at[g], kz_buf.at[g])
         arrived(KZ, kz_buf.at[others_z])
         kc_buf[owner] = jnp.sum(kz_buf[...], axis=0) / nodes
+
+    @pl.when(owns_gram)
+    def _():
+        to_plane(KG, lambda peer, k: kc_buf.at[owner], lambda peer, k: kc_buf.at[owner])
+        arrived(KG, kc_buf.at[pl.ds(0, half - 1)])
+
+    @pl.when(owns_rest)
+    def _():
         to_plane(KC, lambda peer, k: kc_buf.at[owner], lambda peer, k: kc_buf.at[owner])
-        arrived(KC, kc_buf.at[pl.ds(0, n_own - 1)])
-
-    @pl.when(jnp.logical_not(owns))
-    def _():
-        arrived(KC, kc_buf)
-
-    summed = kc_buf[...].reshape(128, 128)
-    inverse = inverse_factor(summed[64:, :64])
+
+    @pl.when(jnp.logical_not(owns_gram))
+    def _():
+        arrived(KG, kc_buf.at[pl.ds(0, half)])
+
+    inverse = inverse_factor(kc_buf[half:].reshape(64, 128)[:, :64])
     v_t = mul(inverse, clean_t)
     v_leaf_t[...] = v_t[:, :leaf_count]
     ends = jnp.concatenate([v_t[:, leaf_count:], jnp.zeros((64, 112), F32)], axis=1)
     ends = jnp.transpose(ends)
     v_sep[...] = ends[0:8]
     v_root[...] = ends[8:16]
-    both = mul(inverse, summed[:64])
+
+    @pl.when(owns_rest)
+    def _():
+        arrived(KC, kc_buf.at[pl.ds(0, half - 1)])
+
+    @pl.when(jnp.logical_not(owns_rest))
+    def _():
+        arrived(KC, kc_buf.at[pl.ds(0, half)])
+
+    both = mul(inverse, kc_buf[:half].reshape(64, 128))
     red_g[...] = mul(both[:, :64], inverse, NT)
     red_c[...] = mul(both[:, 64:], inverse, NT)
 
@@ -437,26 +505,37 @@
     sent(SL, sl_buf.at[others])
     sent(SU, su_buf.at[others])
     sent(SP, sp_buf.at[others])
+    sent(SS, ss_buf.at[others])
     sent(L, l_buf.at[others_z])
     sent(U, u_buf.at[others_z])
     sent(RZ, rz_buf.at[others_z])
     sent(D, d_buf.at[:, others])
     sent(E_, e_buf.at[:, others])
-    sent(F_, f_buf.at[:, others])
-    sent(Z, z_buf.at[others])
-    sent(PR, p_rcv)
-    sent(PZ, pz_buf.at[others_z])
-    sent(PC, pc_buf.at[others])
+    sent(N1, n_rcv)
+    sent(N2, n_buf.at[others])
+    sent(N3, m_src.at[others_z])
+    sent(N4, m_buf.at[others_z])
+    sent(P1, p_rcv)
+    sent(P2, pz_buf.at[others_z])
+    sent(W1, w_rcv)
+    sent(W2, w_buf.at[others])
 
     @pl.when(owns)
     def _():
         sent(KR, k_src.at[pl.ds(0, n_own - 1)])
         sent(KZ, kz_buf.at[others_z])
+
+    @pl.when(jnp.logical_not(owns))
+    def _():
+        sent(KR, k_src)
+
+    @pl.when(owns_gram)
+    def _():
+        sent(KG, k_rcv)
+
+    @pl.when(owns_rest)
+    def _():
         sent(KC, k_rcv)
-
-    @pl.when(jnp.logical_not(owns))
-    def _():
-        sent(KR, k_src)
 
 
 def shards(
@@ -501,17 +580,25 @@
         (n_inner, 8, width),
         (n_inner, 8, 128),
         (n_inner, 8, 128),
+        (n_inner, 8, 128),
+        (n_inner, 8, 128),
         (n_outer, 8, root),
         (n_outer, 8, root),
         (n_outer, n_outer * 4, 128),
         (half, n_inner, 8, 128),
         (half, n_inner, 8, 128),
-        (half, n_inner, 8, 128),
-        (n_inner, 8, 128),
+        (n_inner, 8, basis),
+        (n_inner - 1, 8, basis),
+        (n_inner, 8, basis),
+        (n_outer, 8, basis),
+        (n_outer, 8, basis),
+        (n_outer, 8, basis),
         (n_inner, per, 8, 128),
         (n_inner - 1, per, 8, 128),
         (n_outer, per, 8, 128),
-        (n_inner, per, 8, 128),
+        (n_inner, 1 + per, 8, 128),
+        (n_inner - 1, 1 + per, 8, 128),
+        (n_inner, 1 + per, 8, 128),
         (n_own, per_k, 8, 128),
         (n_inner - 1, per_k, 8, 128),
         (n_outer, per_k, 8, 128),
@@ -544,7 +631,7 @@
         out_specs=[vmem] * 6,
         scratch_shapes=[pltpu.VMEM(s, F32) for s in scratch]
         + [pltpu.VMEM(x.shape, x.dtype) for x in kept]
-        + [pltpu.SemaphoreType.DMA((n,)) for n in (18, 18, 20)],
+        + [pltpu.SemaphoreType.DMA((n,)) for n in (23, 23, 20)],
         compiler_params=pltpu.CompilerParams(
             collective_id=0, has_side_effects=True, vmem_limit_bytes=64 * 2**20
         ),

time: 112 us -> 98.7 us (0.88)
  Pallas kernels: 106 us -> 92.8 us
    pallas_call x1, Pallas kernels: 106 us -> 92.8 us  [shards(): pl.pallas_call(functools.partial(kernel, n_outer, n_inner), out_shape=[ja...]
where the time goes in v3:
time: 98.7 us; the launch traced here: 98.4 us
  Pallas kernels  92.8 us (94%)
  local copies, waits for them, and re-layouts  4.93 us (5%)
    pallas_call x1, Pallas kernels, shards(): pl.pallas_call(functools.partial(kernel, n_outer, n_inner), out_shape=[ja...  92.8 us
    unnamed x16, local copies, waits for them, and re-layouts  4.93 us

profile of v3, /device:TPU:1, one launch (start us, length us, event | category | flops | bytes accessed | tf_op | source)
XLA Modules:
  0.0 98.4 jit_solution(16059670248445192394)
XLA Ops:
  0.6 92.8 %shard_map.235 = (f32[64,256]{1,0:T(8,128)}, f32[8,64]{1,0:T(8,128)}, f32[8,64]{1,0:T(8,128)}, f32[64,512]{1,0:T(8,128)}, f32[64,64]{1,0:T(8,128)}, /*index=5*/f32[64,64]{1,0:T(8,128)}) custom-call(f32[64,256]{1,0:T(8,128)} %bitcast.5, f32[8,64]{1,0:T(8,128)} %h_b_sep.1, f32[8,64]{1,0:T(8,128)} %h_b_root.1, f32[256,256]{1,0:T(8,128)} %h_leaf_linv.1, ...), custom_call_target="tpu_custom_call" | custom-call | tf_op jit(solution)/shard_map/pallas_call | solution.py:627
  93.5 0.0 copy-start
  93.5 0.0 copy-start.4
  93.5 1.5 %copy.32 = f32[256,64]{0,1:T(8,128)} copy(f32[256,64]{0,1:T(8,128)} %bitcast.7) | data formatting | bytes 131072
  95.0 0.0 copy-done.4
  95.0 0.0 copy-start.3
  95.0 0.6 copy.33
  95.6 0.1 copy-done.3
  95.7 0.6 copy.34
  96.3 0.0 copy-done
  96.3 0.0 copy-start.2
  96.3 0.7 copy.35
  96.9 0.1 copy-done.2
  97.0 0.0 copy-start.1
  97.0 0.6 copy.36
  97.6 0.2 copy-done.1
  97.8 0.6 copy.37
Async XLA Ops:
  93.5 2.8 %copy-start = (f32[64,512]{1,0:T(8,128)S(1)}, f32[64,512]{1,0:T(8,128)}, u32[]{:S(2)}) copy-start(f32[64,512]{1,0:T(8,128)} %get-tuple-element.15) | copy-start | bytes 393220
  93.5 1.5 %copy-start.4 = (f32[8,64]{1,0:T(8,128)S(1)}, f32[8,64]{1,0:T(8,128)}, u32[]{:S(2)}) copy-start(f32[8,64]{1,0:T(8,128)} %get-tuple-element.25) | copy-start | bytes 6148
  95.0 0.7 copy-start.3
  96.3 0.8 copy-start.2
  97.0 0.8 copy-start.1

commit v4 on v3

--- a/solution.py
+++ b/solution.py
@@ -43,27 +43,38 @@
     col_ids = lax.broadcasted_iota(jnp.int32, (64, 64), 1)
     start = jnp.concatenate([gram, (row_ids == col_ids).astype(F32)], axis=1)
     groups = tuple(start[8 * a : 8 * a + 8] for a in range(8))
-    sub = lax.broadcasted_iota(jnp.int32, (8, 128), 0)
+
+    def spread(block, k):
+        return jnp.broadcast_to(block[:, k : k + 1], (block.shape[0], 128))
 
     def panel(p, groups):
-        groups = list(groups)
-        scale = jnp.zeros((8, 128), F32)
-        for k in range(8):
-            row = groups[0][k : k + 1, :]
-            pivot = row[:, k : k + 1]
-            scaled = row / pivot
-            for a in range(8):
-                factor = groups[a][:, k : k + 1]
-                if a == 0:
-                    factor = jnp.where(sub > k, jnp.broadcast_to(factor, (8, 128)), 0.0)
-                else:
-                    live = jnp.where(a + p < 8, 1.0, 0.0).astype(F32)
-                    factor = jnp.broadcast_to(factor, (8, 128)) * live
-                groups[a] = groups[a] - factor * scaled
-            scale = jnp.where(sub == k, jnp.broadcast_to(lax.rsqrt(pivot), (8, 128)), scale)
-        groups[0] = groups[0] * scale
-        turned = [pltpu.roll(x, 120, 1) for x in groups]
-        return tuple(turned[1:] + turned[:1])
+        head = groups[0]
+        rows = [head[j : j + 1] for j in range(8)]
+        corner = [[spread(rows[j], k) if k >= j else None for k in range(8)] for j in range(8)]
+        scaled, factors = [], []
+        for j in range(8):
+            inverse = 1.0 / corner[j][j]
+            scaled.append(rows[j] * inverse)
+            factors.append([corner[j][t] * inverse if t > j else None for t in range(8)])
+            for t in range(j + 1, 8):
+                rows[t] = rows[t] - factors[j][t] * rows[j]
+                for k in range(t, 8):
+                    corner[t][k] = corner[t][k] - factors[j][t] * corner[j][k]
+        done = [rows[j] * lax.rsqrt(corner[j][j]) for j in range(8)]
+        turned = []
+        for a in range(1, 8):
+            live = jnp.where(a + p < 8, 1.0, 0.0).astype(F32)
+            columns = []
+            total = jnp.zeros((8, 128), F32)
+            for j in range(8):
+                column = spread(groups[a], j)
+                for t in range(j):
+                    column = column - columns[t] * factors[t][j]
+                columns.append(column)
+                total = total + column * scaled[j]
+            turned.append(groups[a] - live * total)
+        turned.append(jnp.concatenate(done, axis=0))
+        return tuple(pltpu.roll(x, 120, 1) for x in turned)
 
     groups = lax.fori_loop(0, 8, panel, groups)
     return jnp.concatenate(groups, axis=0)[:, :64]
@@ -113,12 +124,12 @@
     h_g_blocks,
     h_c_blocks,
     h_block_cols,
-    v_leaf_t,
-    v_sep,
-    v_root,
-    coef_t,
-    red_g,
-    red_c,
+    o_v_leaf_t,
+    o_v_sep,
+    o_v_root,
+    o_coef_t,
+    o_red_g,
+    o_red_c,
     a_src,
     a_rcv,
     b_buf,
@@ -134,6 +145,8 @@
     d_buf,
     e_buf,
     n_src,
+    n_sib,
+    n_pair,
     n_rcv,
     n_buf,
     m_src,
@@ -165,9 +178,16 @@
     g_blocks,
     c_blocks,
     block_cols,
+    v_leaf_t,
+    v_sep,
+    v_root,
+    coef_t,
+    red_g,
+    red_c,
     send,
     recv,
     here,
+    out,
 ):
     g = lax.axis_index("outer")
     i = lax.axis_index("inner")
@@ -176,7 +196,7 @@
     stride = n_inner // n_own
     leaf_count = h_basis_leaf.shape[0]
     nodes = float(n_outer * n_inner * (leaf_count + 16))
-    A, B, SL, SU, SP, SS, L, U, RZ, D, E_, N1, N2, N3, N4, P1, P2, W1, W2, KR, KZ, KG, KC = range(23)
+    A, B, SL, SU, SP, SS, L, U, RZ, D, E_, N1, N2, N3, N4, P1, P2, W1, W2, KR, KZ, KG, KC, SLB, SUB, N1A, N2B = range(27)
 
     def to_plane(phase, src, dst):
         def one(k, carry):
@@ -193,6 +213,35 @@
 
         lax.fori_loop(1, n_inner, one, 0)
 
+    pairs = n_inner // 2
+    chip, core = i // 2, lax.rem(i, 2)
+    sibling = i + 1 - 2 * core
+
+    def to_same_core(phase, src, dst):
+        def one(k, carry):
+            peer = lax.rem(chip + k, pairs)
+            pltpu.make_async_remote_copy(
+                src_ref=src(peer),
+                dst_ref=dst(k),
+                send_sem=send.at[phase],
+                recv_sem=recv.at[phase],
+                device_id=(g, 2 * peer + core),
+                device_id_type=MESH,
+            ).start()
+            return carry
+
+        lax.fori_loop(1, pairs, one, 0)
+
+    def to_sibling(phase, src, dst):
+        pltpu.make_async_remote_copy(
+            src_ref=src,
+            dst_ref=dst,
+            send_sem=send.at[phase],
+            recv_sem=recv.at[phase],
+            device_id=(g, sibling),
+            device_id_type=MESH,
+        ).start()
+
     def to_column(phase, src, dst):
         def one(k, carry):
             peer = lax.rem(g + k, n_outer)
@@ -215,6 +264,7 @@
         pltpu.make_async_copy(like, like, send.at[phase]).wait()
 
     others = pl.ds(0, n_inner - 1)
+    others_p = pl.ds(0, pairs - 1)
     others_z = pl.ds(0, n_outer - 1)
 
     own_slots = {
@@ -223,10 +273,10 @@
         "leaf_lower": (h_leaf_lower, leaf_lower),
         "sep_rows": (h_sep_rows, sep_rows),
         "sep_lower_t": (h_sep_lower_t, sep_lower_t),
-        "sep_linv": (h_sep_linv, sl_buf.at[i]),
+        "sep_linv": (h_sep_linv, sl_buf.at[chip, core]),
         "root_linv": (h_root_linv, l_buf.at[g]),
         "root_uinv": (h_root_uinv, u_buf.at[g]),
-        "sep_uinv": (h_sep_uinv, su_buf.at[i]),
+        "sep_uinv": (h_sep_uinv, su_buf.at[chip, core]),
         "b_sep": (h_b_sep, b_sep),
         "leaf_uinv": (h_leaf_uinv, leaf_uinv),
         "leaf_upper": (h_leaf_upper, leaf_upper),
@@ -243,6 +293,19 @@
         name: pltpu.make_async_copy(src, dst, here.at[n])
         for n, (name, (src, dst)) in enumerate(own_slots.items())
     }
+    stores = [
+        pltpu.make_async_copy(src, dst, out.at[n])
+        for n, (src, dst) in enumerate(
+            (
+                (v_leaf_t, o_v_leaf_t),
+                (v_sep, o_v_sep),
+                (v_root, o_v_root),
+                (coef_t, o_coef_t),
+                (red_g, o_red_g),
+                (red_c, o_red_c),
+            )
+        )
+    ]
     for load in loads.values():
         load.start()
 
@@ -278,33 +341,38 @@
     contrib_t = mul(y_t, leaf_lower[...], NT)
     update = mul(sel_t, contrib_t, NT)
     a_src[...] = wide(update).reshape(n_inner, 8, 128)
+    loaded("sep_linv", "root_linv", "root_uinv", "sep_uinv", "b_sep")
+
+    pl.semaphore_wait(barrier, n_inner + n_outer - 2)
+
+    to_plane(A, lambda peer, k: a_src.at[peer], lambda peer, k: a_rcv.at[k - 1])
+    to_same_core(SL, lambda peer: sl_buf.at[chip, core], lambda k: sl_buf.at[chip, core])
+    to_column(L, lambda peer: l_buf.at[g], l_buf.at[g])
     loaded("sep_lower_t", "sep_upper")
     by_owner(sep_lower_t[...], n_outer, n_inner, sp_src)
     sp_buf[i] = sp_src[i]
+    to_plane(SP, lambda peer, k: sp_src.at[peer], lambda peer, k: sp_buf.at[i])
     by_owner(sep_upper[...], n_outer, n_inner, ss_src)
     ss_buf[i] = ss_src[i]
-    loaded("sep_linv", "root_linv", "root_uinv", "sep_uinv", "b_sep")
-
-    pl.semaphore_wait(barrier, n_inner + n_outer - 2)
-
-    to_plane(A, lambda peer, k: a_src.at[peer], lambda peer, k: a_rcv.at[k - 1])
-    to_plane(SL, lambda peer, k: sl_buf.at[i], lambda peer, k: sl_buf.at[i])
-    to_plane(SP, lambda peer, k: sp_src.at[peer], lambda peer, k: sp_buf.at[i])
-    to_column(L, lambda peer: l_buf.at[g], l_buf.at[g])
 
     loaded("leaf_uinv", "leaf_upper", "b_root", "basis_leaf", "basis_sep", "basis_root")
     uy_t = mul(y_t, leaf_uinv[...], NT)
     coupling = mul(leaf_uinv[...], mul(leaf_upper[...], sel_t, NT))
     n_src[...] = mul(coupling, q_all[:leaf_count, :], TN).reshape(n_src.shape)
+    to_sibling(N1A, n_src.at[:, 1 - core], n_sib)
 
     arrived(A, a_rcv)
     b_buf[i] = wide(b_sep[...]) - (a_src[i] + jnp.sum(a_rcv[...], axis=0))
     to_plane(B, lambda peer, k: b_buf.at[i], lambda peer, k: b_buf.at[i])
-    to_plane(N1, lambda peer, k: n_src.at[peer], lambda peer, k: n_rcv.at[k - 1])
-    to_plane(SU, lambda peer, k: su_buf.at[i], lambda peer, k: su_buf.at[i])
+    arrived(N1A, n_sib)
+    n_pair[...] = n_src[:, core] + n_sib[...]
+    to_same_core(N1, lambda peer: n_pair.at[peer], lambda k: n_rcv.at[k - 1])
+    arrived(SL, sl_buf.at[others_p, 0])
+    to_sibling(SLB, sl_buf.at[:, core], sl_buf.at[:, core])
+    to_same_core(SU, lambda peer: su_buf.at[chip, core], lambda k: su_buf.at[chip, core])
     to_plane(SS, lambda peer, k: ss_src.at[peer], lambda peer, k: ss_buf.at[i])
 
-    arrived(SL, sl_buf.at[others])
+    arrived(SLB, sl_buf.at[:, 0])
     arrived(SP, sp_buf.at[others])
     sep_inverse = sl_buf[...].reshape(width, width)
     to_root = mul(sp_buf[...].reshape(width, 128)[:, :rb], sep_inverse, TN)
@@ -319,8 +387,11 @@
     to_column(U, lambda peer: u_buf.at[g], u_buf.at[g])
 
     arrived(N1, n_rcv)
-    n_buf[i] = q_all[leaf_count : leaf_count + 8, :] - (n_src[i] + jnp.sum(n_rcv[...], axis=0))
-    to_plane(N2, lambda peer, k: n_buf.at[i], lambda peer, k: n_buf.at[i])
+    mine_n = n_pair[chip] + jnp.sum(n_rcv[...], axis=0)
+    n_buf[chip, core] = q_all[leaf_count : leaf_count + 8, :] - mine_n
+    to_same_core(N2, lambda peer: n_buf.at[chip, core], lambda k: n_buf.at[chip, core])
+    arrived(SU, su_buf.at[others_p, 0])
+    to_sibling(SUB, su_buf.at[:, core], su_buf.at[:, core])
 
     def root_gather(phase, buf, block):
         buf[:, i] = block.reshape(n_outer // 2, 8, 128)
@@ -333,13 +404,13 @@
     arrived(RZ, rz_buf.at[others_z])
     root_gather(D, d_buf, jnp.sum(rz_buf[...], axis=0))
 
-    y_own = mul(sl_buf[i], rhs_sep[:, :64])
+    y_own = mul(sl_buf[chip, core], rhs_sep[:, :64])
     sep_y_t = mul(jnp.transpose(rhs_sep)[:64], sep_inverse, NT)
-    arrived(SU, su_buf.at[others])
+    arrived(SUB, su_buf.at[:, 0])
     sep_upper_inverse = su_buf[...].reshape(width, width)
     from_sep = mul(coupling, sep_upper_inverse)
     start_t = jnp.concatenate(
-        [uy_t - mul(sep_y_t, from_sep, NT), mul(sep_y_t, su_buf[i], NT)], axis=1
+        [uy_t - mul(sep_y_t, from_sep, NT), mul(sep_y_t, su_buf[chip, core], NT)], axis=1
     )
     proj_t = mul(start_t, q_all[: leaf_count + 8, :])
     per = PIECES_P // n_inner
@@ -348,11 +419,13 @@
         p_src[t // per, t % per] = proj_t[8 * r : 8 * r + 8, 128 * c : 128 * c + 128]
     to_plane(P1, lambda peer, k: p_src.at[peer], lambda peer, k: p_rcv.at[k - 1])
 
+    arrived(N2, n_buf.at[others_p, 0])
+    to_sibling(N2B, n_buf.at[:, core], n_buf.at[:, core])
     arrived(SS, ss_buf.at[others])
     sep_by_root = ss_buf[...].reshape(width, 128)[:, :rb]
-    arrived(N2, n_buf.at[others])
+    arrived(N2B, n_buf.at[:, 0])
     m_src[...] = mul(
-        mul(sep_upper_inverse, sep_by_root), n_buf[...].reshape(width, n_buf.shape[2]), TN
+        mul(sep_upper_inverse, sep_by_root), n_buf[...].reshape(width, n_buf.shape[3]), TN
     ).reshape(m_src.shape)
     m_rcv[g] = m_src[g]
     to_column(N3, lambda peer: m_src.at[peer], m_rcv.at[g])
@@ -410,7 +483,7 @@
 
     z_t = jnp.transpose(w_buf[:, 0].reshape(width, 128))[:64]
     x_leaf_t = uy_t - mul(z_t, from_sep, NT)
-    x_sep_t = mul(z_t, su_buf[i], NT)
+    x_sep_t = mul(z_t, su_buf[chip, core], NT)
     x_t = jnp.concatenate([x_leaf_t, x_sep_t, x_root_t], axis=1)
     coefs = jnp.concatenate(
         [
@@ -454,6 +527,7 @@
     to_owners(half)
     clean_leaf_t = clean_t[:, :leaf_count]
     coef_t[...] = coefs
+    stores[3].start()
     g_part = mul(mul(clean_leaf_t, hg[...]), clean_leaf_t, NT)
     c_part = mul(mul(clean_leaf_t, hc[...]), clean_leaf_t, NT)
     k_src[:half] = jnp.concatenate([g_part, c_part], axis=1).reshape(half, per_k, 8, 128)
@@ -483,10 +557,13 @@
     inverse = inverse_factor(kc_buf[half:].reshape(64, 128)[:, :64])
     v_t = mul(inverse, clean_t)
     v_leaf_t[...] = v_t[:, :leaf_count]
+    stores[0].start()
     ends = jnp.concatenate([v_t[:, leaf_count:], jnp.zeros((64, 112), F32)], axis=1)
     ends = jnp.transpose(ends)
     v_sep[...] = ends[0:8]
     v_root[...] = ends[8:16]
+    stores[1].start()
+    stores[2].start()
 
     @pl.when(owns_rest)
     def _():
@@ -498,12 +575,16 @@
 
     both = mul(inverse, kc_buf[:half].reshape(64, 128))
     red_g[...] = mul(both[:, :64], inverse, NT)
+    stores[4].start()
     red_c[...] = mul(both[:, 64:], inverse, NT)
+    stores[5].start()
 
     sent(A, a_rcv)
     sent(B, b_buf.at[others])
-    sent(SL, sl_buf.at[others])
-    sent(SU, su_buf.at[others])
+    sent(SL, sl_buf.at[others_p, 0])
+    sent(SU, su_buf.at[others_p, 0])
+    sent(SLB, sl_buf.at[:, 0])
+    sent(SUB, su_buf.at[:, 0])
     sent(SP, sp_buf.at[others])
     sent(SS, ss_buf.at[others])
     sent(L, l_buf.at[others_z])
@@ -511,8 +592,10 @@
     sent(RZ, rz_buf.at[others_z])
     sent(D, d_buf.at[:, others])
     sent(E_, e_buf.at[:, others])
+    sent(N1A, n_sib)
     sent(N1, n_rcv)
-    sent(N2, n_buf.at[others])
+    sent(N2, n_buf.at[others_p, 0])
+    sent(N2B, n_buf.at[:, 0])
     sent(N3, m_src.at[others_z])
     sent(N4, m_buf.at[others_z])
     sent(P1, p_rcv)
@@ -536,6 +619,23 @@
     @pl.when(owns_rest)
     def _():
         sent(KC, k_rcv)
+
+    for store in stores:
+        store.wait()
+
+
+def hand_over(count, *refs):
+    src, dst, held = refs[:count], refs[count : 2 * count], refs[2 * count : 3 * count]
+    come, go = refs[3 * count :]
+    ins = [pltpu.make_async_copy(src[n], held[n], come.at[n]) for n in range(count)]
+    outs = [pltpu.make_async_copy(held[n], dst[n], go.at[n]) for n in range(count)]
+    for copy in ins:
+        copy.start()
+    for n in range(count):
+        ins[n].wait()
+        outs[n].start()
+    for copy in outs:
+        copy.wait()
 
 
 def shards(
@@ -570,14 +670,13 @@
     per = PIECES_P // n_inner
     n_own = min(PIECES_K, n_inner)
     per_k = PIECES_K // n_own
-    vmem = pl.BlockSpec(memory_space=pltpu.VMEM)
     hbm = pl.BlockSpec(memory_space=pltpu.HBM)
     scratch = [
         (n_inner, 8, 128),
         (n_inner - 1, 8, 128),
         (n_inner, 8, 128),
-        (n_inner, 8, width),
-        (n_inner, 8, width),
+        (n_inner // 2, 2, 8, width),
+        (n_inner // 2, 2, 8, width),
         (n_inner, 8, 128),
         (n_inner, 8, 128),
         (n_inner, 8, 128),
@@ -587,9 +686,11 @@
         (n_outer, n_outer * 4, 128),
         (half, n_inner, 8, 128),
         (half, n_inner, 8, 128),
-        (n_inner, 8, basis),
-        (n_inner - 1, 8, basis),
-        (n_inner, 8, basis),
+        (n_inner // 2, 2, 8, basis),
+        (n_inner // 2, 8, basis),
+        (n_inner // 2, 8, basis),
+        (n_inner // 2 - 1, 8, basis),
+        (n_inner // 2, 2, 8, basis),
         (n_outer, 8, basis),
         (n_outer, 8, basis),
         (n_outer, 8, basis),
@@ -624,14 +725,15 @@
         block_cols,
     )
     outs = [(ports, nodes), (8, ports), (8, ports), (ports, basis), (ports, ports), (ports, ports)]
-    v_leaf_t, v_sep, v_root, coef_t, red_g, red_c = pl.pallas_call(
+    results = pl.pallas_call(
         functools.partial(kernel, n_outer, n_inner),
         out_shape=[jax.ShapeDtypeStruct(s, F32) for s in outs],
         in_specs=[hbm] * 20,
-        out_specs=[vmem] * 6,
+        out_specs=[hbm] * 6,
         scratch_shapes=[pltpu.VMEM(s, F32) for s in scratch]
         + [pltpu.VMEM(x.shape, x.dtype) for x in kept]
-        + [pltpu.SemaphoreType.DMA((n,)) for n in (23, 23, 20)],
+        + [pltpu.VMEM(s, F32) for s in outs]
+        + [pltpu.SemaphoreType.DMA((n,)) for n in (27, 27, 20, 6)],
         compiler_params=pltpu.CompilerParams(
             collective_id=0, has_side_effects=True, vmem_limit_bytes=64 * 2**20
         ),
@@ -657,6 +759,13 @@
         c_blocks,
         block_cols,
     )
+    v_leaf_t, v_sep, v_root, coef_t, red_g, red_c = pl.pallas_call(
+        functools.partial(hand_over, len(outs)),
+        out_shape=[jax.ShapeDtypeStruct(s, F32) for s in outs],
+        in_specs=[hbm] * 6,
+        out_specs=[hbm] * 6,
+        scratch_shapes=[pltpu.VMEM(s, F32) for s in outs] + [pltpu.SemaphoreType.DMA((6,))] * 2,
+    )(*results)
     return v_leaf_t.T, v_sep, v_root, coef_t.T, red_g, red_c
 
 

time: 98.7 us -> 87 us (0.88)
  Pallas kernels: 92.8 us -> 86.3 us
  local copies, waits for them, and re-layouts: 4.93 us -> 0 us
    pallas_call x1, Pallas kernels: 92.8 us -> 84.5 us  [shards(): pl.pallas_call(functools.partial(kernel, n_outer, n_inner), out_shape=[ja...]
    unnamed x16 -> x0, local copies, waits for them, and re-layouts: 4.93 us -> none
    pallas_call x0 -> x1, Pallas kernels: none -> 1.73 us  [shards(): pl.pallas_call(functools.partial(hand_over, len(outs)), out_shape=[jax.Sh...]
where the time goes in v4:
time: 87 us; the launch traced here: 86.9 us
  Pallas kernels  86.3 us (99%)
    pallas_call x1, Pallas kernels, shards(): pl.pallas_call(functools.partial(kernel, n_outer, n_inner), out_shape=[ja...  84.5 us

profile of v4, /device:TPU:1, one launch (start us, length us, event | category | flops | bytes accessed | tf_op | source)
XLA Modules:
  0.0 86.9 jit_solution(7607633592485665891)
XLA Ops:
  0.6 84.5 %shard_map.235 = (f32[64,256]{1,0:T(8,128)}, f32[8,64]{1,0:T(8,128)}, f32[8,64]{1,0:T(8,128)}, f32[64,512]{1,0:T(8,128)}, f32[64,64]{1,0:T(8,128)}, /*index=5*/f32[64,64]{1,0:T(8,128)}) custom-call(f32[64,256]{1,0:T(8,128)} %bitcast.4, f32[8,64]{1,0:T(8,128)} %h_b_sep.1, f32[8,64]{1,0:T(8,128)} %h_b_root.1, f32[256,256]{1,0:T(8,128)} %h_leaf_linv.1, ...), custom_call_target="tpu_custom_call" | custom-call | tf_op jit(solution)/shard_map/pallas_call | solution.py:728
  85.2 1.7 %shard_map.236 = (f32[64,256]{1,0:T(8,128)}, f32[8,64]{1,0:T(8,128)}, f32[8,64]{1,0:T(8,128)}, f32[64,512]{1,0:T(8,128)}, f32[64,64]{1,0:T(8,128)}, /*index=5*/f32[64,64]{1,0:T(8,128)}) custom-call(f32[64,256]{1,0:T(8,128)} %get-tuple-element.18.refs_0_, f32[8,64]{1,0:T(8,128)} %get-tuple-element.19.refs_1_, f32[8,64]{1,0:T(8,128)} %get-tuple-element.20.refs_2_, ...), custom_call_target="tpu_custom_call" | custom-call | tf_op jit(solution)/shard_map/pallas_call | solution.py:762

commit v5 on v4

--- a/solution.py
+++ b/solution.py
@@ -124,12 +124,12 @@
     h_g_blocks,
     h_c_blocks,
     h_block_cols,
-    o_v_leaf_t,
-    o_v_sep,
-    o_v_root,
-    o_coef_t,
-    o_red_g,
-    o_red_c,
+    v_leaf_t,
+    v_sep,
+    v_root,
+    coef_t,
+    red_g,
+    red_c,
     a_src,
     a_rcv,
     b_buf,
@@ -178,16 +178,11 @@
     g_blocks,
     c_blocks,
     block_cols,
-    v_leaf_t,
-    v_sep,
-    v_root,
-    coef_t,
-    red_g,
-    red_c,
     send,
     recv,
     here,
-    out,
+    tri_send,
+    tri_recv,
 ):
     g = lax.axis_index("outer")
     i = lax.axis_index("inner")
@@ -293,19 +288,58 @@
         name: pltpu.make_async_copy(src, dst, here.at[n])
         for n, (name, (src, dst)) in enumerate(own_slots.items())
     }
-    stores = [
-        pltpu.make_async_copy(src, dst, out.at[n])
-        for n, (src, dst) in enumerate(
-            (
-                (v_leaf_t, o_v_leaf_t),
-                (v_sep, o_v_sep),
-                (v_root, o_v_root),
-                (coef_t, o_coef_t),
-                (red_g, o_red_g),
-                (red_c, o_red_c),
-            )
-        )
-    ]
+    span = n_inner * 8
+    for o in range(n_outer):
+        if o + 1 < n_outer:
+            after = (n_outer - 1 - o) * span
+            l_buf[o, :, (o + 1) * span :] = jnp.zeros((8, after), F32)
+        if o:
+            u_buf[o, :, : o * span] = jnp.zeros((8, o * span), F32)
+
+    def part_of(which, o):
+        if which == 0:
+            return l_buf.at[o, :, pl.ds(0, (o + 1) * span)]
+        return u_buf.at[o, :, pl.ds(o * span, (n_outer - o) * span)]
+
+    def triangle_to_column(which):
+        for o in range(n_outer):
+
+            @pl.when(g == o)
+            def _(o=o):
+                def one(k, carry):
+                    pltpu.make_async_remote_copy(
+                        src_ref=part_of(which, o),
+                        dst_ref=part_of(which, o),
+                        send_sem=tri_send.at[which, k],
+                        recv_sem=tri_recv.at[which, o],
+                        device_id=(lax.rem(g + k, n_outer), i),
+                        device_id_type=MESH,
+                    ).start()
+                    return carry
+
+                lax.fori_loop(1, n_outer, one, 0)
+
+    def triangle_arrived(which):
+        for o in range(n_outer):
+
+            @pl.when(g != o)
+            def _(o=o):
+                part = part_of(which, o)
+                pltpu.make_async_copy(part, part, tri_recv.at[which, o]).wait()
+
+    def triangle_sent(which):
+        for o in range(n_outer):
+
+            @pl.when(g == o)
+            def _(o=o):
+                part = part_of(which, o)
+
+                def one(k, carry):
+                    pltpu.make_async_copy(part, part, tri_send.at[which, k]).wait()
+                    return carry
+
+                lax.fori_loop(1, n_outer, one, 0)
+
     for load in loads.values():
         load.start()
 
@@ -347,7 +381,7 @@
 
     to_plane(A, lambda peer, k: a_src.at[peer], lambda peer, k: a_rcv.at[k - 1])
     to_same_core(SL, lambda peer: sl_buf.at[chip, core], lambda k: sl_buf.at[chip, core])
-    to_column(L, lambda peer: l_buf.at[g], l_buf.at[g])
+    triangle_to_column(0)
     loaded("sep_lower_t", "sep_upper")
     by_owner(sep_lower_t[...], n_outer, n_inner, sp_src)
     sp_buf[i] = sp_src[i]
@@ -384,7 +418,7 @@
     own = jnp.where(mine, jnp.concatenate([b_root[...]] * n_outer, axis=0), 0.0)
     rz_buf[g] = folded(own - part)
     to_column(RZ, lambda peer: rz_buf.at[g], rz_buf.at[g])
-    to_column(U, lambda peer: u_buf.at[g], u_buf.at[g])
+    triangle_to_column(1)
 
     arrived(N1, n_rcv)
     mine_n = n_pair[chip] + jnp.sum(n_rcv[...], axis=0)
@@ -430,7 +464,7 @@
     m_rcv[g] = m_src[g]
     to_column(N3, lambda peer: m_src.at[peer], m_rcv.at[g])
 
-    arrived(L, l_buf.at[others_z])
+    triangle_arrived(0)
     lower_rows = l_buf[...].reshape(rb, l_buf.shape[2])
     y_root = unfolded_product(lower_rows, root_value(D, d_buf))
     root_gather(E_, e_buf, folded(y_root))
@@ -458,7 +492,7 @@
     arrived(P2, pz_buf.at[others_z])
     proj_start = jnp.sum(pz_buf[...], axis=0)
 
-    arrived(U, u_buf.at[others_z])
+    triangle_arrived(1)
     upper_rows = u_buf[...].reshape(rb, u_buf.shape[2])
     x_root = unfolded_product(upper_rows, root_value(E_, e_buf))
 
@@ -527,7 +561,6 @@
     to_owners(half)
     clean_leaf_t = clean_t[:, :leaf_count]
     coef_t[...] = coefs
-    stores[3].start()
     g_part = mul(mul(clean_leaf_t, hg[...]), clean_leaf_t, NT)
     c_part = mul(mul(clean_leaf_t, hc[...]), clean_leaf_t, NT)
     k_src[:half] = jnp.concatenate([g_part, c_part], axis=1).reshape(half, per_k, 8, 128)
@@ -557,13 +590,10 @@
     inverse = inverse_factor(kc_buf[half:].reshape(64, 128)[:, :64])
     v_t = mul(inverse, clean_t)
     v_leaf_t[...] = v_t[:, :leaf_count]
-    stores[0].start()
     ends = jnp.concatenate([v_t[:, leaf_count:], jnp.zeros((64, 112), F32)], axis=1)
     ends = jnp.transpose(ends)
     v_sep[...] = ends[0:8]
     v_root[...] = ends[8:16]
-    stores[1].start()
-    stores[2].start()
 
     @pl.when(owns_rest)
     def _():
@@ -575,9 +605,7 @@
 
     both = mul(inverse, kc_buf[:half].reshape(64, 128))
     red_g[...] = mul(both[:, :64], inverse, NT)
-    stores[4].start()
     red_c[...] = mul(both[:, 64:], inverse, NT)
-    stores[5].start()
 
     sent(A, a_rcv)
     sent(B, b_buf.at[others])
@@ -587,8 +615,8 @@
     sent(SUB, su_buf.at[:, 0])
     sent(SP, sp_buf.at[others])
     sent(SS, ss_buf.at[others])
-    sent(L, l_buf.at[others_z])
-    sent(U, u_buf.at[others_z])
+    triangle_sent(0)
+    triangle_sent(1)
     sent(RZ, rz_buf.at[others_z])
     sent(D, d_buf.at[:, others])
     sent(E_, e_buf.at[:, others])
@@ -620,21 +648,15 @@
     def _():
         sent(KC, k_rcv)
 
-    for store in stores:
-        store.wait()
-
 
 def hand_over(count, *refs):
-    src, dst, held = refs[:count], refs[count : 2 * count], refs[2 * count : 3 * count]
-    come, go = refs[3 * count :]
-    ins = [pltpu.make_async_copy(src[n], held[n], come.at[n]) for n in range(count)]
-    outs = [pltpu.make_async_copy(held[n], dst[n], go.at[n]) for n in range(count)]
-    for copy in ins:
+    done = refs[-1]
+    copies = [
+        pltpu.make_async_copy(refs[n], refs[count + n], done.at[n]) for n in range(count)
+    ]
+    for copy in copies:
         copy.start()
-    for n in range(count):
-        ins[n].wait()
-        outs[n].start()
-    for copy in outs:
+    for copy in copies:
         copy.wait()
 
 
@@ -725,19 +747,20 @@
         block_cols,
     )
     outs = [(ports, nodes), (8, ports), (8, ports), (ports, basis), (ports, ports), (ports, ports)]
+    vmem = pl.BlockSpec(memory_space=pltpu.VMEM)
     results = pl.pallas_call(
         functools.partial(kernel, n_outer, n_inner),
-        out_shape=[jax.ShapeDtypeStruct(s, F32) for s in outs],
+        out_shape=[pltpu.VMEM(s, F32) for s in outs],
         in_specs=[hbm] * 20,
-        out_specs=[hbm] * 6,
+        out_specs=[vmem] * 6,
         scratch_shapes=[pltpu.VMEM(s, F32) for s in scratch]
         + [pltpu.VMEM(x.shape, x.dtype) for x in kept]
-        + [pltpu.VMEM(s, F32) for s in outs]
-        + [pltpu.SemaphoreType.DMA((n,)) for n in (27, 27, 20, 6)],
+        + [pltpu.SemaphoreType.DMA((n,)) for n in (27, 27, 20)]
+        + [pltpu.SemaphoreType.DMA((2, n_outer))] * 2,
         compiler_params=pltpu.CompilerParams(
-            collective_id=0, has_side_effects=True, vmem_limit_bytes=64 * 2**20
+            collective_id=0, has_side_effects=True, vmem_limit_bytes=58 * 2**20
         ),
-    )(
+    )(*(pltpu.with_memory_space_constraint(x, pltpu.HBM) for x in (
         b_leaf_t,
         b_sep,
         b_root,
@@ -758,13 +781,14 @@
         g_blocks,
         c_blocks,
         block_cols,
-    )
+    )))
     v_leaf_t, v_sep, v_root, coef_t, red_g, red_c = pl.pallas_call(
         functools.partial(hand_over, len(outs)),
         out_shape=[jax.ShapeDtypeStruct(s, F32) for s in outs],
-        in_specs=[hbm] * 6,
+        in_specs=[vmem] * 6,
         out_specs=[hbm] * 6,
-        scratch_shapes=[pltpu.VMEM(s, F32) for s in outs] + [pltpu.SemaphoreType.DMA((6,))] * 2,
+        scratch_shapes=[pltpu.SemaphoreType.DMA((6,))],
+        compiler_params=pltpu.CompilerParams(vmem_limit_bytes=8 * 2**20),
     )(*results)
     return v_leaf_t.T, v_sep, v_root, coef_t.T, red_g, red_c
 

time: 87 us -> 84.9 us (0.976)
  Pallas kernels: 86.3 us -> 84.1 us
    pallas_call x1, Pallas kernels: 84.5 us -> 83.4 us  [shards(): pl.pallas_call(functools.partial(kernel, n_outer, n_inner), out_shape=[pl...]
    pallas_call x1, Pallas kernels: 1.73 us -> 0.75 us  [shards(): pl.pallas_call(functools.partial(hand_over, len(outs)), out_shape=[jax.Sh...]
where the time goes in v5:
time: 84.9 us; the launch traced here: 84.8 us
  Pallas kernels  84.1 us (99%)
    pallas_call x1, Pallas kernels, shards(): pl.pallas_call(functools.partial(kernel, n_outer, n_inner), out_shape=[pl...  83.4 us

profile of v5, /device:TPU:1, one launch (start us, length us, event | category | flops | bytes accessed | tf_op | source)
XLA Modules:
  0.0 84.8 jit_solution(17983753437614752191)
XLA Ops:
  0.6 83.4 %shard_map.235 = (f32[64,256]{1,0:T(8,128)S(1)}, f32[8,64]{1,0:T(8,128)S(1)}, f32[8,64]{1,0:T(8,128)S(1)}, f32[64,512]{1,0:T(8,128)S(1)}, f32[64,64]{1,0:T(8,128)S(1)}, /*index=5*/f32[64,64]{1,0:T(8,128)S(1)}) custom-call(f32[64,256]{1,0:T(8,128)} %bitcast.4, f32[8,64]{1,0:T(8,128)} %h_b_sep.1, f32[8,64]{1,0:T(8,128)} %h_b_root.1, f32[256,256]{1,0:T(8,128)} %h_leaf_linv.1, ...), custom_call_target="tpu_custom_call" | custom-call | tf_op jit(solution)/shard_map/pallas_call | solution.py:751
  84.0 0.8 shard_map.236

commit v6 on v5

--- a/solution.py
+++ b/solution.py
@@ -99,6 +99,11 @@
             for o in range(1, n_outer):
                 total = jnp.where(lane_group == (ii + o) % 16, shifted[o], total)
             out_ref[16 * m + ii] = pltpu.roll(total, 128 - ii * 8, 1) if ii else total
+
+
+def around(count, far, body):
+    lax.fori_loop(far, count, body, 0)
+    lax.fori_loop(1, far, body, 0)
 
 
 def kernel(
@@ -193,6 +198,8 @@
     nodes = float(n_outer * n_inner * (leaf_count + 16))
     A, B, SL, SU, SP, SS, L, U, RZ, D, E_, N1, N2, N3, N4, P1, P2, W1, W2, KR, KZ, KG, KC, SLB, SUB, N1A, N2B = range(27)
 
+    far_plane, far_chip, far_column = n_inner * 5 // 8, max(n_inner * 5 // 16, 1), max(n_outer * 3 // 8, 1)
+
     def to_plane(phase, src, dst):
         def one(k, carry):
             peer = lax.rem(i + k, n_inner)
@@ -206,7 +213,7 @@
             ).start()
             return carry
 
-        lax.fori_loop(1, n_inner, one, 0)
+        around(n_inner, far_plane, one)
 
     pairs = n_inner // 2
     chip, core = i // 2, lax.rem(i, 2)
@@ -225,7 +232,7 @@
             ).start()
             return carry
 
-        lax.fori_loop(1, pairs, one, 0)
+        around(pairs, far_chip, one)
 
     def to_sibling(phase, src, dst):
         pltpu.make_async_remote_copy(
@@ -250,7 +257,7 @@
             ).start()
             return carry
 
-        lax.fori_loop(1, n_outer, one, 0)
+        around(n_outer, far_column, one)
 
     def arrived(phase, like):
         pltpu.make_async_copy(like, like, recv.at[phase]).wait()
@@ -361,7 +368,7 @@
         )
         return carry
 
-    lax.fori_loop(1, n_inner, greet_plane, 0)
+    around(n_inner, far_plane, greet_plane)
     lax.fori_loop(1, n_outer, greet_column, 0)
 
     loaded("b_t", "leaf_linv", "leaf_lower", "sep_rows")
@@ -420,6 +427,8 @@
     to_column(RZ, lambda peer: rz_buf.at[g], rz_buf.at[g])
     triangle_to_column(1)
 
+    y_own = mul(sl_buf[chip, core], rhs_sep[:, :64])
+    sep_y_t = mul(jnp.transpose(rhs_sep)[:64], sep_inverse, NT)
     arrived(N1, n_rcv)
     mine_n = n_pair[chip] + jnp.sum(n_rcv[...], axis=0)
     n_buf[chip, core] = q_all[leaf_count : leaf_count + 8, :] - mine_n
@@ -438,8 +447,6 @@
     arrived(RZ, rz_buf.at[others_z])
     root_gather(D, d_buf, jnp.sum(rz_buf[...], axis=0))
 
-    y_own = mul(sl_buf[chip, core], rhs_sep[:, :64])
-    sep_y_t = mul(jnp.transpose(rhs_sep)[:64], sep_inverse, NT)
     arrived(SUB, su_buf.at[:, 0])
     sep_upper_inverse = su_buf[...].reshape(width, width)
     from_sep = mul(coupling, sep_upper_inverse)
@@ -538,15 +545,15 @@
     owns_rest = jnp.logical_and(owns, owner < half)
 
     def to_owners(first):
-        def one(k, carry):
-            peer = lax.rem(i + k, n_inner)
-            at = peer // stride
-
-            @pl.when(jnp.logical_and(lax.rem(peer, stride) == 0, at // half == first // half))
+        def one(n, carry):
+            at = first + n
+            peer = at * stride
+
+            @pl.when(peer != i)
             def _():
                 pltpu.make_async_remote_copy(
                     src_ref=k_src.at[at],
-                    dst_ref=k_rcv.at[k - 1],
+                    dst_ref=k_rcv.at[lax.rem(peer + n_inner - i, n_inner) - 1],
                     send_sem=send.at[KR],
                     recv_sem=recv.at[KR],
                     device_id=(g, peer),
@@ -555,7 +562,7 @@
 
             return carry
 
-        lax.fori_loop(1, n_inner, one, 0)
+        lax.fori_loop(0, half, one, 0)
 
     k_src[half:] = wide(mul(clean_t, clean_t, NT)).reshape(half, per_k, 8, 128)
     to_owners(half)

time: 84.9 us -> 83.2 us (0.980)
  Pallas kernels: 84.1 us -> 82.5 us
    pallas_call x1, Pallas kernels: 83.4 us -> 81.7 us  [shards(): pl.pallas_call(functools.partial(kernel, n_outer, n_inner), out_shape=[pl...]
where the time goes in v6:
time: 83.2 us; the launch traced here: 83.1 us
  Pallas kernels  82.5 us (99%)
    pallas_call x1, Pallas kernels, shards(): pl.pallas_call(functools.partial(kernel, n_outer, n_inner), out_shape=[pl...  81.7 us

profile of v6, /device:TPU:1, one launch (start us, length us, event | category | flops | bytes accessed | tf_op | source)
XLA Modules:
  0.0 83.1 jit_solution(18059707983406101632)
XLA Ops:
  0.6 81.7 %shard_map.235 = (f32[64,256]{1,0:T(8,128)S(1)}, f32[8,64]{1,0:T(8,128)S(1)}, f32[8,64]{1,0:T(8,128)S(1)}, f32[64,512]{1,0:T(8,128)S(1)}, f32[64,64]{1,0:T(8,128)S(1)}, /*index=5*/f32[64,64]{1,0:T(8,128)S(1)}) custom-call(f32[64,256]{1,0:T(8,128)} %bitcast.4, f32[8,64]{1,0:T(8,128)} %h_b_sep.1, f32[8,64]{1,0:T(8,128)} %h_b_root.1, f32[256,256]{1,0:T(8,128)} %h_leaf_linv.1, ...), custom_call_target="tpu_custom_call" | custom-call | tf_op jit(solution)/shard_map/pallas_call | solution.py:758
  82.4 0.8 shard_map.236

commit v7 on v6

--- a/solution.py
+++ b/solution.py
@@ -295,6 +295,27 @@
         name: pltpu.make_async_copy(src, dst, here.at[n])
         for n, (name, (src, dst)) in enumerate(own_slots.items())
     }
+    first = ("b_t", "leaf_linv", "leaf_lower", "sep_rows")
+    for name in first:
+        loads[name].start()
+
+    barrier = pltpu.get_barrier_semaphore()
+
+    def greet_plane(k, carry):
+        pl.semaphore_signal(
+            barrier, inc=1, device_id=(g, lax.rem(i + k, n_inner)), device_id_type=MESH
+        )
+        return carry
+
+    def greet_column(k, carry):
+        pl.semaphore_signal(
+            barrier, inc=1, device_id=(lax.rem(g + k, n_outer), i), device_id_type=MESH
+        )
+        return carry
+
+    around(n_inner, far_plane, greet_plane)
+    lax.fori_loop(1, n_outer, greet_column, 0)
+
     span = n_inner * 8
     for o in range(n_outer):
         if o + 1 < n_outer:
@@ -347,31 +368,15 @@
 
                 lax.fori_loop(1, n_outer, one, 0)
 
-    for load in loads.values():
-        load.start()
+    for name, load in loads.items():
+        if name not in first:
+            load.start()
 
     def loaded(*names):
         for name in names:
             loads[name].wait()
 
-    barrier = pltpu.get_barrier_semaphore()
-
-    def greet_plane(k, carry):
-        pl.semaphore_signal(
-            barrier, inc=1, device_id=(g, lax.rem(i + k, n_inner)), device_id_type=MESH
-        )
-        return carry
-
-    def greet_column(k, carry):
-        pl.semaphore_signal(
-            barrier, inc=1, device_id=(lax.rem(g + k, n_outer), i), device_id_type=MESH
-        )
-        return carry
-
-    around(n_inner, far_plane, greet_plane)
-    lax.fori_loop(1, n_outer, greet_column, 0)
-
-    loaded("b_t", "leaf_linv", "leaf_lower", "sep_rows")
+    loaded(*first)
     width = n_inner * 8
     couples = sep_rows.shape[1]
     sel_t = (
@@ -450,16 +455,6 @@
     arrived(SUB, su_buf.at[:, 0])
     sep_upper_inverse = su_buf[...].reshape(width, width)
     from_sep = mul(coupling, sep_upper_inverse)
-    start_t = jnp.concatenate(
-        [uy_t - mul(sep_y_t, from_sep, NT), mul(sep_y_t, su_buf[chip, core], NT)], axis=1
-    )
-    proj_t = mul(start_t, q_all[: leaf_count + 8, :])
-    per = PIECES_P // n_inner
-    for t in range(PIECES_P):
-        r, c = t // 4, t % 4
-        p_src[t // per, t % per] = proj_t[8 * r : 8 * r + 8, 128 * c : 128 * c + 128]
-    to_plane(P1, lambda peer, k: p_src.at[peer], lambda peer, k: p_rcv.at[k - 1])
-
     arrived(N2, n_buf.at[others_p, 0])
     to_sibling(N2B, n_buf.at[:, core], n_buf.at[:, core])
     arrived(SS, ss_buf.at[others])
@@ -470,6 +465,16 @@
     ).reshape(m_src.shape)
     m_rcv[g] = m_src[g]
     to_column(N3, lambda peer: m_src.at[peer], m_rcv.at[g])
+
+    start_t = jnp.concatenate(
+        [uy_t - mul(sep_y_t, from_sep, NT), mul(sep_y_t, su_buf[chip, core], NT)], axis=1
+    )
+    proj_t = mul(start_t, q_all[: leaf_count + 8, :])
+    per = PIECES_P // n_inner
+    for t in range(PIECES_P):
+        r, c = t // 4, t % 4
+        p_src[t // per, t % per] = proj_t[8 * r : 8 * r + 8, 128 * c : 128 * c + 128]
+    to_plane(P1, lambda peer, k: p_src.at[peer], lambda peer, k: p_rcv.at[k - 1])
 
     triangle_arrived(0)
     lower_rows = l_buf[...].reshape(rb, l_buf.shape[2])

time: 83.2 us -> 82.8 us (level)
  no operation moved by 1% of the time
where the time goes in v7:
time: 82.8 us; the launch traced here: 82.7 us
  Pallas kernels  82 us (99%)
    pallas_call x1, Pallas kernels, shards(): pl.pallas_call(functools.partial(kernel, n_outer, n_inner), out_shape=[pl...  81.3 us

profile of v7, /device:TPU:1, one launch (start us, length us, event | category | flops | bytes accessed | tf_op | source)
XLA Modules:
  0.0 82.7 jit_solution(726322655795883352)
XLA Ops:
  0.6 81.3 %shard_map.235 = (f32[64,256]{1,0:T(8,128)S(1)}, f32[8,64]{1,0:T(8,128)S(1)}, f32[8,64]{1,0:T(8,128)S(1)}, f32[64,512]{1,0:T(8,128)S(1)}, f32[64,64]{1,0:T(8,128)S(1)}, /*index=5*/f32[64,64]{1,0:T(8,128)S(1)}) custom-call(f32[64,256]{1,0:T(8,128)} %bitcast.4, f32[8,64]{1,0:T(8,128)} %h_b_sep.1, f32[8,64]{1,0:T(8,128)} %h_b_root.1, f32[256,256]{1,0:T(8,128)} %h_leaf_linv.1, ...), custom_call_target="tpu_custom_call" | custom-call | tf_op jit(solution)/shard_map/pallas_call | solution.py:763
  81.9 0.8 shard_map.236
